TPU v7x, 256 devices: a whole 4x4x8 slice. The times are simulated.
256 devices in a mesh: sec: 64 (over z, x, core), pair: 4 (over y).
Axes of the slice: x: 4, y: 4, z: 8, core: 2. Of those that a mesh axis runs over, the one named last changes fastest.
Arguments:
- psi_start: float32 [64, 16, 128, 128], P('sec', 'pair'), may hold values from -6 to 6
- left_env: float32 [6, 64, 128, 128], P(None, 'sec')
- right_env: float32 [6, 16, 128, 128], P(None, 'pair')
- mpo_coef: float32 [6, 16, 16], replicated, may hold values from -0.625 to 0.625
- mpo_pattern: int32 [6, 16, 16], replicated, may hold values 0 or 1
- sector_shift: int32 [6], replicated, may hold values from -1 to 1, as said below
- block_rows: int32 [64], P('sec'), may hold values from 64 to 128, as said below
Outputs:
- state: float32 [64, 16, 128, 128], P('sec', 'pair')
- energies: float32 [4], replicated
Inputs may be any that keep to these rules, and one draw needn't show every extreme that they name: `sector_shift`: each of -1, 0 and 1 occurs at least once. `block_rows`: some sector has all 128 rows.
All inputs are finite; a program needn't handle non-finite values.
Results may differ from a plain program's by a relative error of at most 0.0013.
Values sent between devices are 32-bit elements; how exact they have to be, the bound alone decides.
No kernel may reach another device: no remote copies, remote signals or barrier semaphores. Data moves between devices by JAX's collectives and lax.ppermute only.
A program may use at most 192 MiB of HBM per device.

v0:
```python
import jax
import jax.numpy as jnp
from jax import lax
from jax.sharding import PartitionSpec as P

ITERS = 4


precise = lax.Precision.HIGHEST


def padded(block, sides, width):
    for axis, dim in sides:
        count = lax.axis_size(axis)
        forward = [(i, i + 1) for i in range(count - 1)]
        backward = [(target, source) for source, target in forward]
        low = lax.ppermute(
            lax.slice_in_dim(block, block.shape[dim] - width, None, axis=dim), axis, forward
        )
        high = lax.ppermute(lax.slice_in_dim(block, 0, width, axis=dim), axis, backward)
        block = jnp.concatenate([low, block, high], axis=dim)
    return block


def mix_channels(full, right_all, weights_local):
    right_part = jnp.einsum("sqij,kqlj->ksqil", full, right_all, precision=precise)
    return jnp.einsum("kpq,ksqil->kspil", weights_local, right_part, precision=precise)


def apply_ham(vector, left_env, right_all, weights_local, sector_shift, mask):
    sectors = vector.shape[0]
    full = lax.all_gather(vector, "pair", axis=1, tiled=True)
    mixed = mix_channels(full, right_all, weights_local)
    extended = padded(mixed, (("sec", 1),), 1)
    total = jnp.zeros(vector.shape, jnp.float32)
    for term in range(left_env.shape[0]):
        source = lax.dynamic_slice_in_dim(extended[term], sector_shift[term] + 1, sectors, 0)
        total = total + jnp.einsum("sil,splj->spij", left_env[term], source, precision=precise)
    return total * mask[:, None, :, None]


def ritz_stats(state, image, count):
    sums = lax.psum((jnp.sum(state * image), jnp.sum(state * state)), ("sec", "pair"))
    return (sums[0] / count, sums[1] / count)


def lowest_root(lead, middle, const):
    root = jnp.sqrt(middle * middle - 4.0 * lead * const)
    return jnp.where(middle > 0, (-middle - root) / (2.0 * lead), 2.0 * const / (root - middle))


def on_device(psi_start, left_env, right_env, mpo_coef, mpo_pattern, sector_shift, block_rows):
    blocks = psi_start.shape[2]
    local_channels = psi_start.shape[1]
    count = float(psi_start.size * lax.axis_size("sec") * lax.axis_size("pair"))
    first = lax.axis_index("pair") * local_channels
    mask = (jnp.arange(blocks)[None, :] < block_rows[:, None]).astype(jnp.float32)
    weights = mpo_coef * mpo_pattern.astype(jnp.float32)
    weights_local = lax.dynamic_slice_in_dim(weights, first, local_channels, 1)
    right_all = lax.all_gather(right_env, "pair", axis=1, tiled=True)
    chosen = (sector_shift == 0).astype(jnp.float32)
    weight_diag = lax.dynamic_slice_in_dim(
        jnp.diagonal(weights, axis1=1, axis2=2), first, local_channels, 1
    )
    weight_diag = weight_diag * chosen[:, None]
    left_diag = jnp.diagonal(left_env, axis1=2, axis2=3)
    right_diag = jnp.diagonal(right_env, axis1=2, axis2=3)
    diag = jnp.einsum("kp,ksi,kpj->spij", weight_diag, left_diag, right_diag, precision=precise)
    diag = diag * mask[:, None, :, None]
    state = psi_start * mask[:, None, :, None]
    image = apply_ham(state, left_env, right_all, weights_local, sector_shift, mask)
    energies = []
    lowest = jnp.float32(0.0)
    for step in range(ITERS):
        rayleigh, length = ritz_stats(state, image, count)
        theta = rayleigh / length
        correction = (image - theta * state) / jnp.maximum(jnp.abs(diag - theta), 1.0)
        image_corr = apply_ham(correction, left_env, right_all, weights_local, sector_shift, mask)
        sums = lax.psum(
            (
                jnp.sum(state * image_corr),
                jnp.sum(correction * image),
                jnp.sum(correction * image_corr),
                jnp.sum(state * correction),
                jnp.sum(correction * correction),
            ),
            ("sec", "pair"),
        )
        cross = 0.5 * (sums[0] + sums[1]) / count
        curvature = sums[2] / count
        correlation = sums[3] / count
        spread = sums[4] / count
        lead = length * spread - correlation * correlation
        middle = -(length * curvature + spread * rayleigh - 2.0 * correlation * cross)
        const = rayleigh * curvature - cross * cross
        lowest = lowest_root(lead, middle, const)
        keep = curvature - lowest * spread
        add = lowest * correlation - cross
        factor = 1.0 / jnp.sqrt(
            keep * keep * length + 2.0 * keep * add * correlation + add * add * spread
        )
        state = (keep * state + add * correction) * factor
        image = (keep * image + add * image_corr) * factor
        energies.append(lowest)
    return (state, jnp.stack(energies))


def solution(mesh):
    in_specs = (
        P("sec", "pair", None, None),
        P(None, "sec", None, None),
        P(None, "pair", None, None),
        P(),
        P(),
        P(),
        P("sec"),
    )
    out_specs = (P("sec", "pair", None, None), P())
    return jax.shard_map(
        on_device, mesh=mesh, in_specs=in_specs, out_specs=out_specs, check_vma=False
    )
```

profile of v0, /device:TPU:1, one launch (start us, length us, event | category | flops | bytes accessed | tf_op | source)
XLA Modules:
  0.0 1133.0 jit_solution(3367695057665482696)
XLA Ops:
  12.7 27.1 %all-gather.7.cloned.1.call-done = f32[1,16,128,128]{3,2,0,1:T(8,128)} async-done(((f32[1,4,128,128]{3,2,0,1:T(8,128)}), f32[1,16,128,128]{3,2,0,1:T(8,128)}) %all-gather.7.cloned.1.call-update) | async-done | bytes 1048592 | tf_op jit(solution)/shard_map/all_gather | solution.py:32
  39.9 71.3 %all-gather.9.cloned.1.call-done = f32[6,16,128,128]{3,2,0,1:T(8,128)} async-done(((f32[6,4,128,128]{3,2,0,1:T(8,128)}), f32[6,16,128,128]{3,2,0,1:T(8,128)}) %all-gather.9.cloned.1.call-update) | async-done | bytes 6291472 | tf_op jit(solution)/shard_map/all_gather | solution.py:60
  111.2 7.8 convolution_bitcast_fusion.4
  119.0 6.7 fusion.10
  139.9 16.9 %copy.168 = f32[6,4,128,128]{0,1,3,2:T(4,128)} copy(f32[6,4,128,128]{3,2,1,0:T(8,128)S(1)} %copy-done.1) | data formatting | bytes 3145728 | tf_op args[2]
  157.0 4.7 copy.165
  174.3 79.0 %all-reduce.7 = (f32[]{:T(128)}, f32[]{:T(128)}) all-reduce(f32[]{:T(128)} %get-tuple-element.31, f32[]{:T(128)} %get-tuple-element.30), channel_id=1, replica_groups=mesh['sec'=64,'pair'=4] {'sec','pair'}, use_global_device_ids=true, to_apply=%region_1.2 | all-reduce | flops 2 | bytes 16 | tf_op jit(solution)/shard_map/psum | solution.py:43
  256.3 21.5 %all-gather.11.cloned.1.call-done = f32[1,16,128,128]{3,2,0,1:T(8,128)} async-done(((f32[1,4,128,128]{3,2,0,1:T(8,128)}), f32[1,16,128,128]{3,2,0,1:T(8,128)}) %all-gather.11.cloned.1.call-update) | async-done | bytes 1048592 | tf_op jit(solution)/shard_map/all_gather | solution.py:32
  277.8 7.8 convolution_bitcast_fusion.3
  285.6 7.0 fusion.13
  299.6 15.7 %collective-permute-done.3 = f32[6,1,4,128,128]{4,2,3,0,1:T(4,128)S(1)} collective-permute-done((f32[6,1,4,128,128]{4,2,3,0,1:T(4,128)S(1)}, f32[6,1,4,128,128]{4,2,3,0,1:T(4,128)S(1)}, u32[]{:S(2)}, u32[]{:S(2)}) %collective-permute-start.3) | collective-permute-done | bytes 1572896 | tf_op jit(solution)/shard_map/ppermute | solution.py:20
  324.1 79.5 %all-reduce.6 = (f32[]{:T(128)}, f32[]{:T(128)}, f32[]{:T(128)}, f32[]{:T(128)}) all-reduce(f32[]{:T(128)} %get-tuple-element.28, f32[]{:T(128)} %get-tuple-element.29, f32[]{:T(128)} %get-tuple-element.26, f32[]{:T(128)S(6)} %add.447), channel_id=1, replica_groups=mesh['sec'=64,'pair'=4] {'sec','pair'}, use_global_device_ids=true, to_apply=%region_5.6 | all-reduce | flops 4 | bytes 32 | tf_op jit(solution)/shard_map/psum | solution.py:79
  416.0 74.0 %all-reduce.5 = (f32[]{:T(128)}, f32[]{:T(128)}) all-reduce(f32[]{:T(128)} %get-tuple-element.24, f32[]{:T(128)} %get-tuple-element.23), channel_id=1, replica_groups=mesh['sec'=64,'pair'=4] {'sec','pair'}, use_global_device_ids=true, to_apply=%region_15.16 | all-reduce | flops 2 | bytes 16 | tf_op jit(solution)/shard_map/psum | solution.py:43
  492.5 21.7 %all-gather.13.cloned.1.call-done = f32[1,16,128,128]{3,2,0,1:T(8,128)} async-done(((f32[1,4,128,128]{3,2,0,1:T(8,128)}), f32[1,16,128,128]{3,2,0,1:T(8,128)}) %all-gather.13.cloned.1.call-update) | async-done | bytes 1048592 | tf_op jit(solution)/shard_map/all_gather | solution.py:32
  514.2 7.8 convolution_bitcast_fusion.2
  522.0 7.0 fusion.16
  529.0 3.5 collective-permute-start.5
  535.7 15.9 %collective-permute-done.5 = f32[6,1,4,128,128]{4,2,3,0,1:T(4,128)S(1)} collective-permute-done((f32[6,1,4,128,128]{4,2,3,0,1:T(4,128)S(1)}, f32[6,1,4,128,128]{4,2,3,0,1:T(4,128)S(1)}, u32[]{:S(2)}, u32[]{:S(2)}) %collective-permute-start.5) | collective-permute-done | bytes 1572896 | tf_op jit(solution)/shard_map/ppermute | solution.py:20
  560.5 79.5 %all-reduce.4 = (f32[]{:T(128)}, f32[]{:T(128)}, f32[]{:T(128)}, f32[]{:T(128)}) all-reduce(f32[]{:T(128)} %get-tuple-element.21, f32[]{:T(128)} %get-tuple-element.22, f32[]{:T(128)} %get-tuple-element.19, f32[]{:T(128)S(6)} %add.460), channel_id=1, replica_groups=mesh['sec'=64,'pair'=4] {'sec','pair'}, use_global_device_ids=true, to_apply=%region_19.20 | all-reduce | flops 4 | bytes 32 | tf_op jit(solution)/shard_map/psum | solution.py:79
  652.2 74.0 %all-reduce.3 = (f32[]{:T(128)}, f32[]{:T(128)}) all-reduce(f32[]{:T(128)} %get-tuple-element.17, f32[]{:T(128)} %get-tuple-element.16), channel_id=1, replica_groups=mesh['sec'=64,'pair'=4] {'sec','pair'}, use_global_device_ids=true, to_apply=%region_29.30 | all-reduce | flops 2 | bytes 16 | tf_op jit(solution)/shard_map/psum | solution.py:43
  728.8 21.7 %all-gather.15.cloned.1.call-done = f32[1,16,128,128]{3,2,0,1:T(8,128)} async-done(((f32[1,4,128,128]{3,2,0,1:T(8,128)}), f32[1,16,128,128]{3,2,0,1:T(8,128)}) %all-gather.15.cloned.1.call-update) | async-done | bytes 1048592 | tf_op jit(solution)/shard_map/all_gather | solution.py:32
  750.4 7.8 convolution_bitcast_fusion.1
  758.2 7.0 fusion.19
  772.2 15.7 %collective-permute-done.7 = f32[6,1,4,128,128]{4,2,3,0,1:T(4,128)S(1)} collective-permute-done((f32[6,1,4,128,128]{4,2,3,0,1:T(4,128)S(1)}, f32[6,1,4,128,128]{4,2,3,0,1:T(4,128)S(1)}, u32[]{:S(2)}, u32[]{:S(2)}) %collective-permute-start.7) | collective-permute-done | bytes 1572896 | tf_op jit(solution)/shard_map/ppermute | solution.py:20
  796.7 79.5 %all-reduce.2 = (f32[]{:T(128)}, f32[]{:T(128)}, f32[]{:T(128)}, f32[]{:T(128)}) all-reduce(f32[]{:T(128)} %get-tuple-element.14, f32[]{:T(128)} %get-tuple-element.15, f32[]{:T(128)} %get-tuple-element.12, f32[]{:T(128)S(6)} %add.473), channel_id=1, replica_groups=mesh['sec'=64,'pair'=4] {'sec','pair'}, use_global_device_ids=true, to_apply=%region_33.34 | all-reduce | flops 4 | bytes 32 | tf_op jit(solution)/shard_map/psum | solution.py:79
  888.6 74.2 %all-reduce.1 = (f32[]{:T(128)}, f32[]{:T(128)}) all-reduce(f32[]{:T(128)} %get-tuple-element.10, f32[]{:T(128)} %get-tuple-element.9), channel_id=1, replica_groups=mesh['sec'=64,'pair'=4] {'sec','pair'}, use_global_device_ids=true, to_apply=%region_43.44 | all-reduce | flops 2 | bytes 16 | tf_op jit(solution)/shard_map/psum | solution.py:43
  965.0 22.0 %all-gather.17.cloned.1.call-done = f32[1,16,128,128]{3,2,0,1:T(8,128)} async-done(((f32[1,4,128,128]{3,2,0,1:T(8,128)}), f32[1,16,128,128]{3,2,0,1:T(8,128)}) %all-gather.17.cloned.1.call-update) | async-done | bytes 1048592 | tf_op jit(solution)/shard_map/all_gather | solution.py:32
  987.0 7.8 convolution_bitcast_fusion
  994.8 7.0 fusion.22
  1001.8 3.5 collective-permute-start.9
  1008.5 15.9 %collective-permute-done.9 = f32[6,1,4,128,128]{4,2,3,0,1:T(4,128)S(1)} collective-permute-done((f32[6,1,4,128,128]{4,2,3,0,1:T(4,128)S(1)}, f32[6,1,4,128,128]{4,2,3,0,1:T(4,128)S(1)}, u32[]{:S(2)}, u32[]{:S(2)}) %collective-permute-start.9) | collective-permute-done | bytes 1572896 | tf_op jit(solution)/shard_map/ppermute | solution.py:20
  1033.3 79.5 %all-reduce = (f32[]{:T(128)}, f32[]{:T(128)}, f32[]{:T(128)}, f32[]{:T(128)}) all-reduce(f32[]{:T(128)} %get-tuple-element.7, f32[]{:T(128)} %get-tuple-element.8, f32[]{:T(128)} %get-tuple-element.5, f32[]{:T(128)S(6)} %add.486), channel_id=1, replica_groups=mesh['sec'=64,'pair'=4] {'sec','pair'}, use_global_device_ids=true, to_apply=%region_47.48 | all-reduce | flops 4 | bytes 32 | tf_op jit(solution)/shard_map/psum | solution.py:79
  (133 shorter events, 82.4 us)
Async XLA Ops:
  7.2 5.5 copy-start.2
  7.2 5.5 copy-start.3
  7.2 32.7 %all-gather.7.cloned.1.call-start = ((), (), s32[]{:S(2)}) async-start(), calls=%async_computation | async-start | bytes 1310720 | tf_op jit(solution)/shard_map/all_gather | solution.py:32
  9.9 101.3 %all-gather.9.cloned.1.call-start = ((), (), s32[]{:S(2)}) async-start(), calls=%async_computation.1 | async-start | bytes 7864320 | tf_op jit(solution)/shard_map/all_gather | solution.py:60
  12.7 265.1 %all-gather.11.cloned.1.call-start = ((), (), s32[]{:S(2)}) async-start(), calls=%async_computation.2 | async-start | bytes 1310720 | tf_op jit(solution)/shard_map/all_gather | solution.py:32
  119.0 12.6 %copy-start.4 = (s32[6]{0:T(128)S(1)}, s32[6]{0:T(128)}, u32[]{:S(2)}) copy-start(s32[6]{0:T(128)} %param.12) | copy-start | bytes 76
  119.0 20.9 %copy-start.1 = (f32[6,4,128,128]{3,2,1,0:T(8,128)S(1)}, f32[6,4,128,128]{3,2,1,0:T(8,128)}, u32[]{:S(2)}) copy-start(f32[6,4,128,128]{3,2,1,0:T(8,128)} %param.9) | copy-start | bytes 4718596
  125.8 40.4 %collective-permute-start.1 = (f32[6,1,4,128,128]{4,2,3,0,1:T(4,128)}, f32[6,1,4,128,128]{4,2,3,0,1:T(4,128)}, u32[]{:S(2)}, u32[]{:S(2)}) collective-permute-start(f32[6,1,4,128,128]{4,2,3,0,1:T(4,128)} %fusion.10), channel_id=1, source_target_pairs={{4,0},{8,4},{12,8},{16,12},{20,16},{24,20},{28,24},{32,28},{36,32}... | collective-permute-start | bytes 4718600 | tf_op jit(solution)/shard_map/ppermute | solution.py:20
  128.4 37.8 %collective-permute-start = (f32[6,1,4,128,128]{4,2,3,0,1:T(4,128)}, f32[6,1,4,128,128]{4,2,3,0,1:T(4,128)}, u32[]{:S(2)}, u32[]{:S(2)}) collective-permute-start(f32[6,1,4,128,128]{4,2,3,0,1:T(4,128)} %fusion.10), channel_id=1, source_target_pairs={{0,4},{4,8},{8,12},{12,16},{16,20},{20,24},{24,28},{28,32},{32,36}... | collective-permute-start | bytes 4718600 | tf_op jit(solution)/shard_map/ppermute | solution.py:17
  139.9 17.1 %copy-start = (f32[6,1,128,128]{3,2,1,0:T(8,128)S(1)}, f32[6,1,128,128]{3,2,1,0:T(8,128)}, u32[]{:S(2)}) copy-start(f32[6,1,128,128]{3,2,1,0:T(8,128)} %param.8) | copy-start | bytes 1179652
  256.0 258.2 %all-gather.13.cloned.1.call-start = ((), (), s32[]{:S(2)}) async-start(), calls=%async_computation.3 | async-start | bytes 1310720 | tf_op jit(solution)/shard_map/all_gather | solution.py:32
  292.6 22.7 %collective-permute-start.3 = (f32[6,1,4,128,128]{4,2,3,0,1:T(4,128)S(1)}, f32[6,1,4,128,128]{4,2,3,0,1:T(4,128)S(1)}, u32[]{:S(2)}, u32[]{:S(2)}) collective-permute-start(f32[6,1,4,128,128]{4,2,3,0,1:T(4,128)S(1)} %fusion.13), channel_id=1, source_target_pairs={{4,0},{8,4},{12,8},{16,12},{20,16},{24,20},{28,24},{32,28},{36,32}... | collective-permute-start | bytes 4718600 | tf_op jit(solution)/shard_map/ppermute | solution.py:20
  296.1 20.3 %collective-permute-start.2 = (f32[6,1,4,128,128]{4,2,3,0,1:T(4,128)S(1)}, f32[6,1,4,128,128]{4,2,3,0,1:T(4,128)S(1)}, u32[]{:S(2)}, u32[]{:S(2)}) collective-permute-start(f32[6,1,4,128,128]{4,2,3,0,1:T(4,128)S(1)} %fusion.13), channel_id=1, source_target_pairs={{0,4},{4,8},{8,12},{12,16},{16,20},{20,24},{24,28},{28,32},{32,36}... | collective-permute-start | bytes 4718600 | tf_op jit(solution)/shard_map/ppermute | solution.py:17
  492.2 258.2 %all-gather.15.cloned.1.call-start = ((), (), s32[]{:S(2)}) async-start(), calls=%async_computation.4 | async-start | bytes 1310720 | tf_op jit(solution)/shard_map/all_gather | solution.py:32
  529.0 22.7 %collective-permute-start.5 = (f32[6,1,4,128,128]{4,2,3,0,1:T(4,128)S(1)}, f32[6,1,4,128,128]{4,2,3,0,1:T(4,128)S(1)}, u32[]{:S(2)}, u32[]{:S(2)}) collective-permute-start(f32[6,1,4,128,128]{4,2,3,0,1:T(4,128)S(1)} %fusion.16), channel_id=1, source_target_pairs={{4,0},{8,4},{12,8},{16,12},{20,16},{24,20},{28,24},{32,28},{36,32}... | collective-permute-start | bytes 4718600 | tf_op jit(solution)/shard_map/ppermute | solution.py:20
  532.5 20.3 %collective-permute-start.4 = (f32[6,1,4,128,128]{4,2,3,0,1:T(4,128)S(1)}, f32[6,1,4,128,128]{4,2,3,0,1:T(4,128)S(1)}, u32[]{:S(2)}, u32[]{:S(2)}) collective-permute-start(f32[6,1,4,128,128]{4,2,3,0,1:T(4,128)S(1)} %fusion.16), channel_id=1, source_target_pairs={{0,4},{4,8},{8,12},{12,16},{16,20},{20,24},{24,28},{28,32},{32,36}... | collective-permute-start | bytes 4718600 | tf_op jit(solution)/shard_map/ppermute | solution.py:17
  728.5 258.6 %all-gather.17.cloned.1.call-start = ((), (), s32[]{:S(2)}) async-start(), calls=%async_computation.5 | async-start | bytes 1310720 | tf_op jit(solution)/shard_map/all_gather | solution.py:32
  765.2 22.7 %collective-permute-start.7 = (f32[6,1,4,128,128]{4,2,3,0,1:T(4,128)S(1)}, f32[6,1,4,128,128]{4,2,3,0,1:T(4,128)S(1)}, u32[]{:S(2)}, u32[]{:S(2)}) collective-permute-start(f32[6,1,4,128,128]{4,2,3,0,1:T(4,128)S(1)} %fusion.19), channel_id=1, source_target_pairs={{4,0},{8,4},{12,8},{16,12},{20,16},{24,20},{28,24},{32,28},{36,32}... | collective-permute-start | bytes 4718600 | tf_op jit(solution)/shard_map/ppermute | solution.py:20
  768.7 20.3 %collective-permute-start.6 = (f32[6,1,4,128,128]{4,2,3,0,1:T(4,128)S(1)}, f32[6,1,4,128,128]{4,2,3,0,1:T(4,128)S(1)}, u32[]{:S(2)}, u32[]{:S(2)}) collective-permute-start(f32[6,1,4,128,128]{4,2,3,0,1:T(4,128)S(1)} %fusion.19), channel_id=1, source_target_pairs={{0,4},{4,8},{8,12},{12,16},{16,20},{20,24},{24,28},{28,32},{32,36}... | collective-permute-start | bytes 4718600 | tf_op jit(solution)/shard_map/ppermute | solution.py:17
  1001.8 22.7 %collective-permute-start.9 = (f32[6,1,4,128,128]{4,2,3,0,1:T(4,128)S(1)}, f32[6,1,4,128,128]{4,2,3,0,1:T(4,128)S(1)}, u32[]{:S(2)}, u32[]{:S(2)}) collective-permute-start(f32[6,1,4,128,128]{4,2,3,0,1:T(4,128)S(1)} %fusion.22), channel_id=1, source_target_pairs={{4,0},{8,4},{12,8},{16,12},{20,16},{24,20},{28,24},{32,28},{36,32}... | collective-permute-start | bytes 4718600 | tf_op jit(solution)/shard_map/ppermute | solution.py:20
  1005.3 20.3 %collective-permute-start.8 = (f32[6,1,4,128,128]{4,2,3,0,1:T(4,128)S(1)}, f32[6,1,4,128,128]{4,2,3,0,1:T(4,128)S(1)}, u32[]{:S(2)}, u32[]{:S(2)}) collective-permute-start(f32[6,1,4,128,128]{4,2,3,0,1:T(4,128)S(1)} %fusion.22), channel_id=1, source_target_pairs={{0,4},{4,8},{8,12},{12,16},{16,20},{20,24},{24,28},{28,32},{32,36}... | collective-permute-start | bytes 4718600 | tf_op jit(solution)/shard_map/ppermute | solution.py:17
Sparse Core Ops, SparseCore 0:
  10.4 29.4 all-gather.6
  41.7 69.4 all-gather.8
  256.1 21.6 all-gather.10
  492.4 21.8 all-gather.12
  728.6 21.8 all-gather.14
  965.1 21.8 all-gather.16
where the time goes:
time: 1140 us; the launch traced here: 1130 us
  blocking collectives  619 us (54%)
  waiting for transfers between devices  253 us (22%)
  matrix products  95.2 us (8%)
  between operations  80.2 us (7%)
  local copies, waits for them, and re-layouts  38 us (3%)
  starting transfers between devices  34 us (3%)
  other arithmetic  12.6 us (1%)
    psum x4, blocking collectives, on_device(): lax.psum((jnp.sum(state * image_corr), jnp.sum(correction * image), jnp.s...  318 us
    psum x4, blocking collectives, ritz_stats(): lax.psum((jnp.sum(state * image), jnp.sum(state * state)), ('sec', 'pair'))  301 us
    all_gather x5, waiting for transfers between devices, apply_ham(): full = lax.all_gather(vector, 'pair', axis=1, tiled=True)  114 us
    all_gather x1, waiting for transfers between devices, on_device(): right_all = lax.all_gather(right_env, 'pair', axis=1, tiled=True)  71.3 us
    ppermute x5, waiting for transfers between devices, padded(): lax.ppermute(lax.slice_in_dim(block, 0, width, axis=dim), axis, backward)  63.3 us
    dot_general x5, matrix products, mix_channels(): jnp.einsum('sqij,kqlj->ksqil', full, right_all, precision=precise)  39 us
    dot_general x5, matrix products, mix_channels(): jnp.einsum('kpq,ksqil->kspil', weights_local, right_part, precision=precise)  34.7 us
    unnamed x15, local copies, waits for them, and re-layouts  26.2 us
  transfers between devices with their start and end apart: 16, of which 14 were waited for; matrix products, arithmetic and copies ran while one was open for 3% of the time, Pallas kernels for 0%

commit v1 on v0

v1 whole, which is shorter than its diff:
```python
import jax
import jax.numpy as jnp
from jax import lax
from jax.experimental import pallas as pl
from jax.experimental.pallas import tpu as pltpu
from jax.sharding import PartitionSpec as P

ITERS = 4
TERMS = 6
LOCAL = 4
GROUPS = 4
B = 128
PACK = LOCAL * B + 8

f32 = jnp.float32
bf16 = jnp.bfloat16
VM = pl.BlockSpec(memory_space=pltpu.VMEM)
SM = pl.BlockSpec(memory_space=pltpu.SMEM)
PARAMS = pltpu.CompilerParams(vmem_limit_bytes=48 * 1024 * 1024)


def halves(x):
    high = x.astype(bf16)
    return high, (x - high.astype(f32)).astype(bf16)


def eye_mask():
    return lax.broadcasted_iota(jnp.int32, (B, B), 0) == lax.broadcasted_iota(jnp.int32, (B, B), 1)


def pack_kernel(shift, rows, psi, left, pack):
    keep = (lax.broadcasted_iota(jnp.int32, (B, B), 0) < rows[0]).astype(f32)
    for p in range(LOCAL):
        pack[p * B:(p + 1) * B, :] = psi[p] * keep
    eye = eye_mask()
    lines = []
    for k in range(TERMS):
        chosen = jnp.where(shift[k] == 0, 1.0, 0.0).astype(f32)
        diag = jnp.sum(jnp.where(eye, left[k] * keep, 0.0), axis=0, keepdims=True)
        lines.append(diag * chosen)
    lines.append(jnp.zeros((8 - TERMS, B), f32))
    pack[LOCAL * B:PACK, :] = jnp.concatenate(lines, axis=0)


def split_kernel(group, rows, weights, left, right, left2, right2, right_diag):
    keep = (lax.broadcasted_iota(jnp.int32, (B, B), 0) < rows[0]).astype(f32)
    eye = eye_mask()
    for k in range(TERMS):
        left2[k] = jnp.concatenate(halves(left[k] * keep), axis=1)
    for q in range(LOCAL):
        lines = []
        for k in range(TERMS):
            block = right[k, q]
            right2[k, q] = jnp.concatenate(halves(jnp.transpose(block)), axis=1)
            p = group[0] * LOCAL + q
            scale = weights[k * 256 + p * 16 + p]
            lines.append(jnp.sum(jnp.where(eye, block, 0.0), axis=0, keepdims=True) * scale)
        lines.append(jnp.zeros((8 - TERMS, B), f32))
        right_diag[q] = jnp.concatenate(lines, axis=0)


def partial_images(group, shift, weights, left2, right2, vec2, z, outs):
    def term(k, carry):
        source = shift[k] + 1
        lhs = left2[k]
        for q in range(LOCAL):
            r = right2[k, q]
            x = jnp.dot(vec2[source, q], jnp.concatenate([r, r], axis=0), preferred_element_type=f32)
            xh, xl = halves(x[:, :B] + x[:, B:])
            both = jnp.concatenate([xh, xl], axis=1)
            y = jnp.dot(lhs, jnp.concatenate([both, both], axis=0), preferred_element_type=f32)
            z[k * LOCAL + q] = y[:, :B] + y[:, B:]
        return carry

    lax.fori_loop(0, TERMS, term, 0)
    for step, out in enumerate(outs):
        base = lax.rem(group[0] + step, GROUPS) * LOCAL

        def pair(t, carry, out=out, base=base):
            first = base + 2 * t
            acc = [jnp.zeros((B, B), f32), jnp.zeros((B, B), f32)]
            for k in range(TERMS):
                for q in range(LOCAL):
                    block = z[k * LOCAL + q]
                    for j in range(2):
                        at = k * 256 + (first + j) * 16 + group[0] * LOCAL + q
                        acc[j] = acc[j] + weights[at] * block
            for j in range(2):
                out[2 * t + j] = acc[j]
            return carry

        lax.fori_loop(0, LOCAL // 2, pair, 0)


def first_kernel(group, shift, weights, pack, pack_low, pack_high, left2, right2, right_diag,
                 state3, diag3, out0, out1, out2, out3, vec2, z):
    for sector, src in enumerate((pack_low, pack, pack_high)):
        lines = src[LOCAL * B:PACK, :]
        for p in range(LOCAL):
            block = src[p * B:(p + 1) * B, :]
            state3[sector, p] = block
            vec2[sector, p] = jnp.concatenate(halves(block), axis=1)
            diag3[sector, p] = lax.dot_general(
                lines, right_diag[p], (((0,), (0,)), ((), ())),
                precision=lax.Precision.HIGHEST, preferred_element_type=f32)
    partial_images(group, shift, weights, left2, right2, vec2, z, (out0, out1, out2, out3))


def lane(row, j):
    at = lax.broadcasted_iota(jnp.int32, row.shape, 1) == j
    return jnp.sum(jnp.where(at, row, 0.0), axis=1, keepdims=True)


def put_lanes(values):
    at = lax.broadcasted_iota(jnp.int32, (1, B), 1)
    row = jnp.zeros((1, B), f32)
    for j, v in enumerate(values):
        row = jnp.where(at == j, v, row)
    return row


def lowest_root(lead, middle, const):
    root = jnp.sqrt(middle * middle - 4.0 * lead * const)
    return jnp.where(middle > 0, (-middle - root) / (2.0 * lead), 2.0 * const / (root - middle))


def ritz(sums, rayleigh, length):
    s_ic, c_i, curvature, correlation, spread = sums
    cross = 0.5 * (s_ic + c_i)
    lead = length * spread - correlation * correlation
    middle = -(length * curvature + spread * rayleigh - 2.0 * correlation * cross)
    const = rayleigh * curvature - cross * cross
    lowest = lowest_root(lead, middle, const)
    keep = curvature - lowest * spread
    add = lowest * correlation - cross
    norm = keep * keep * length + 2.0 * keep * add * correlation + add * add * spread
    factor = 1.0 / jnp.sqrt(norm)
    keep, add = keep * factor, add * factor
    rayleigh = keep * keep * rayleigh + 2.0 * keep * add * cross + add * add * curvature
    length = keep * keep * length + 2.0 * keep * add * correlation + add * add * spread
    return lowest, keep, add, rayleigh, length


def totals(stats, count, n):
    row = jnp.sum(stats[...], axis=0, keepdims=True) * (1.0 / count)
    return [lane(row, j) for j in range(n)]


def correct(state, image, diag, theta):
    return (image - theta * state) / jnp.maximum(jnp.abs(diag - theta), 1.0)


def start_kernel(count, group, shift, weights, stats, state3, diag3, image, image_low, image_high, left2, right2,
                 corr3, carry, out0, out1, out2, out3, vec2, z):
    rayleigh, length = totals(stats, count, 2)
    theta = rayleigh / length
    for sector, src in enumerate((image_low, image, image_high)):
        for p in range(LOCAL):
            c = correct(state3[sector, p], src[p], diag3[sector, p], theta)
            corr3[sector, p] = c
            vec2[sector, p] = jnp.concatenate(halves(c), axis=1)
    carry[...] = jnp.broadcast_to(put_lanes([rayleigh, length]), (8, B))
    partial_images(group, shift, weights, left2, right2, vec2, z, (out0, out1, out2, out3))


def next_kernel(count, step, group, shift, weights, stats, carry_in, state3, diag3, corr3,
                im_low, im_own, im_high, add_low, add_own, add_high, left2, right2,
                state_out, image_out, corr_out, carry, out0, out1, out2, out3, vec2, z):
    sums = totals(stats, count, 5)
    old = carry_in[0:1, :]
    lowest, keep, add, rayleigh, length = ritz(sums, lane(old, 0), lane(old, 1))
    theta = rayleigh / length
    images = ((im_low, add_low), (im_own, add_own), (im_high, add_high))
    for sector, (im, more) in enumerate(images):
        for p in range(LOCAL):
            s = keep * state3[sector, p] + add * corr3[sector, p]
            i = keep * im[p] + add * more[p]
            c = correct(s, i, diag3[sector, p], theta)
            state_out[sector, p] = s
            image_out[sector, p] = i
            corr_out[sector, p] = c
            vec2[sector, p] = jnp.concatenate(halves(c), axis=1)
    energies = [lane(old, 2 + j) for j in range(step)] + [lowest]
    carry[...] = jnp.broadcast_to(put_lanes([rayleigh, length] + energies), (8, B))
    partial_images(group, shift, weights, left2, right2, vec2, z, (out0, out1, out2, out3))


def last_kernel(count, stats, carry_in, state, corr, state_out, energies):
    sums = totals(stats, count, 5)
    old = carry_in[0:1, :]
    lowest, keep, add, _, _ = ritz(sums, lane(old, 0), lane(old, 1))
    for p in range(LOCAL):
        state_out[p] = keep * state[0, p] + add * corr[0, p]
    row = put_lanes([lane(old, 2 + j) for j in range(ITERS - 1)] + [lowest])
    energies[...] = row


def sum_all(block):
    return jnp.sum(jnp.sum(block, axis=0, keepdims=True), axis=1, keepdims=True)


def first_stats_kernel(own, r1, r2, r3, state, image, stats):
    a, b = jnp.zeros((B, B), f32), jnp.zeros((B, B), f32)
    for p in range(LOCAL):
        i = (own[p] + r2[p]) + (r1[p] + r3[p])
        s = state[0, p]
        image[p] = i
        a = a + s * i
        b = b + s * s
    stats[...] = jnp.broadcast_to(put_lanes([sum_all(a), sum_all(b)]), stats.shape)


def stats_kernel(own, r1, r2, r3, state, corr, image, image_corr, stats):
    acc = [jnp.zeros((B, B), f32) for _ in range(5)]
    for p in range(LOCAL):
        ic = (own[p] + r2[p]) + (r1[p] + r3[p])
        s, c, i = state[0, p], corr[0, p], image[0, p]
        image_corr[p] = ic
        for j, v in enumerate((s * ic, c * i, c * ic, s * c, c * c)):
            acc[j] = acc[j] + v
    stats[...] = jnp.broadcast_to(put_lanes([sum_all(a) for a in acc]), stats.shape)


def arr(*shape, dtype=f32):
    return jax.ShapeDtypeStruct(shape, dtype)


BLOCK = arr(LOCAL, B, B)
BLOCK3 = arr(3, LOCAL, B, B)
SCRATCH = [pltpu.VMEM((3, LOCAL, B, 2 * B), bf16), pltpu.VMEM((TERMS * LOCAL, B, B), f32)]


def call(kernel, name, in_specs, outs, scratch=()):
    return pl.pallas_call(
        kernel,
        grid=(1,),
        out_shape=outs,
        in_specs=in_specs,
        out_specs=[VM] * len(outs),
        scratch_shapes=list(scratch),
        compiler_params=PARAMS,
        name=name,
    )


def ring(n, step):
    return [(i, (i + step) % n) for i in range(n)]


def reduce_pair(parts):
    return [lax.ppermute(parts[d], "pair", ring(GROUPS, d)) for d in (1, 2, 3)]


def from_neighbours(x):
    n = lax.axis_size("sec")
    low = lax.ppermute(x, "sec", [(i, i + 1) for i in range(n - 1)])
    high = lax.ppermute(x, "sec", [(i + 1, i) for i in range(n - 1)])
    return low, high


def exchange(stats, devices):
    got = lax.all_to_all(stats.reshape(devices, 1, B), ("sec", "pair"), 0, 0)
    return got.reshape(devices, B)


def middle(arity):
    return [pl.BlockSpec((1, LOCAL, B, B), lambda i: (1, 0, 0, 0))] * arity


def on_device(psi_start, left_env, right_env, mpo_coef, mpo_pattern, sector_shift, block_rows):
    devices = lax.axis_size("sec") * lax.axis_size("pair")
    count = float(psi_start.size * devices)
    psi = psi_start.reshape(LOCAL, B, B)
    left = left_env.reshape(TERMS, B, B)
    group = lax.axis_index("pair").astype(jnp.int32).reshape(1)
    weights = (mpo_coef * mpo_pattern.astype(f32)).reshape(-1)
    stats_shape = arr(devices, B)
    carry_shape = arr(8, B)
    parts = [BLOCK] * 4

    (pack,) = call(pack_kernel, "pack", [SM, SM, VM, VM], [arr(PACK, B)])(sector_shift, block_rows, psi, left)
    pack_low, pack_high = from_neighbours(pack)
    left2, right2, right_diag = call(
        split_kernel, "split", [SM, SM, SM, VM, VM],
        [arr(TERMS, B, 2 * B, dtype=bf16), arr(TERMS, LOCAL, B, 2 * B, dtype=bf16), arr(LOCAL, 8, B)],
    )(group, block_rows, weights, left, right_env)

    state3, diag3, *out = call(
        first_kernel, "first", [SM] * 3 + [VM] * 6, [BLOCK3, BLOCK3] + parts, SCRATCH
    )(group, sector_shift, weights, pack, pack_low, pack_high, left2, right2, right_diag)
    got = reduce_pair(out)
    image, stats = call(
        first_stats_kernel, "first_stats", [VM] * 4 + middle(1), [BLOCK, stats_shape]
    )(out[0], *got, state3)
    image_low, image_high = from_neighbours(image)
    stats = exchange(stats, devices)

    corr3, carry, *out = call(
        lambda *refs: start_kernel(count, *refs), "start", [SM] * 3 + [VM] * 8, [BLOCK3, carry_shape] + parts, SCRATCH
    )(group, sector_shift, weights, stats, state3, diag3, image, image_low, image_high, left2, right2)
    images = (image_low, image, image_high)
    image_own, own_spec = image.reshape(1, LOCAL, B, B), [pl.BlockSpec((1, LOCAL, B, B), lambda i: (0, 0, 0, 0))]

    for step in range(ITERS):
        got = reduce_pair(out)
        image_corr, stats = call(
            stats_kernel, "stats", [VM] * 4 + middle(2) + own_spec, [BLOCK, stats_shape]
        )(out[0], *got, state3, corr3, image_own)
        if step == ITERS - 1:
            break
        low, high = from_neighbours(image_corr)
        stats = exchange(stats, devices)
        if step == 0:
            im_specs, im_args = [VM] * 3, images
        else:
            im_specs = [pl.BlockSpec((None, LOCAL, B, B), lambda i, j=j: (j, 0, 0, 0)) for j in range(3)]
            im_args = (image3, image3, image3)
        state3, image3, corr3, carry, *out = call(
            lambda *refs, step=step: next_kernel(count, step, *refs), "next",
            [SM] * 3 + [VM] * 5 + im_specs + [VM] * 5, [BLOCK3] * 3 + [carry_shape] + parts, SCRATCH,
        )(group, sector_shift, weights, stats, carry, state3, diag3, corr3, *im_args, low, image_corr, high,
          left2, right2)
        image_own, own_spec = image3, middle(1)

    stats = exchange(stats, devices)
    state, energies = call(
        lambda *refs: last_kernel(count, *refs), "last", [VM] * 2 + middle(2), [BLOCK, arr(1, B)]
    )(stats, carry, state3, corr3)
    return state.reshape(psi_start.shape), energies[0, :ITERS]


def solution(mesh):
    in_specs = (
        P("sec", "pair", None, None),
        P(None, "sec", None, None),
        P(None, "pair", None, None),
        P(),
        P(),
        P(),
        P("sec"),
    )
    out_specs = (P("sec", "pair", None, None), P())
    return jax.shard_map(
        on_device, mesh=mesh, in_specs=in_specs, out_specs=out_specs, check_vma=False
    )
```

time: 1140 us -> 269 us (0.24)
  blocking collectives: 619 us -> 117 us
  waiting for transfers between devices: 253 us -> 56.7 us
  matrix products: 95.2 us -> 0 us
  between operations: 80.2 us -> 1.61 us
  Pallas kernels: 0 us -> 38.9 us
  local copies, waits for them, and re-layouts: 38 us -> 5.63 us
  starting transfers between devices: 34 us -> 47 us
  other arithmetic: 12.6 us -> 0.83 us
    psum x8 -> x0, blocking collectives: 619 us -> none  [the longest x4 318 us: on_device(): lax.psum((jnp.sum(state * image_corr), jnp.sum(correction * image), jnp.s...]
    all_gather x6 -> x0, waiting for transfers between devices: 185 us -> none  [the longest x5 114 us: apply_ham(): full = lax.all_gather(vector, 'pair', axis=1, tiled=True)]
    all_to_all x0 -> x5, blocking collectives: none -> 117 us  [exchange(): got = lax.all_to_all(stats.reshape(devices, 1, B), ('sec', 'pair'), 0, 0)]
    dot_general x41 -> x0, matrix products: 95.2 us -> none  [the longest x5 39 us: mix_channels(): jnp.einsum('sqij,kqlj->ksqil', full, right_all, precision=precise)]
    pallas_call x0 -> x13, Pallas kernels: none -> 38.9 us  [the longest x3 22 us: on_device(): call(lambda *refs, step=step: next_kernel(count, step, *refs), 'next', [S...]
    unnamed x15 -> x28, local copies, waits for them, and re-layouts: 26.2 us -> 5.04 us
    ppermute x10 -> x25, starting transfers between devices: 33.1 us -> 47 us  [the longest x5 18.1 us: from_neighbours(): high = lax.ppermute(x, 'sec', [(i + 1, i) for i in range(n - 1)])]
    ppermute x10 -> x25, waiting for transfers between devices: 68 us -> 56.7 us  [the longest x15 56.7 us: reduce_pair(): return [lax.ppermute(parts[d], 'pair', ring(GROUPS, d)) for d in (1, 2, 3)]]
  transfers between devices with their start and end apart: 16 -> 25, of which waited for: 14 -> 14; matrix products, arithmetic and copies ran while one was open for 3% -> 0% of each run, Pallas kernels for 0% -> 0%
where the time goes in v1:
time: 269 us; the launch traced here: 268 us
  blocking collectives  117 us (43%)
  waiting for transfers between devices  56.7 us (21%)
  starting transfers between devices  47 us (17%)
  Pallas kernels  38.9 us (14%)
  local copies, waits for them, and re-layouts  5.63 us (2%)
    all_to_all x5, blocking collectives, exchange(): got = lax.all_to_all(stats.reshape(devices, 1, B), ('sec', 'pair'), 0, 0)  117 us
    ppermute x15, waiting for transfers between devices, reduce_pair(): return [lax.ppermute(parts[d], 'pair', ring(GROUPS, d)) for d in (1, 2, 3)]  56.7 us
    pallas_call x3, Pallas kernels, on_device(): call(lambda *refs, step=step: next_kernel(count, step, *refs), 'next', [S...  22 us
    ppermute x5, starting transfers between devices, from_neighbours(): high = lax.ppermute(x, 'sec', [(i + 1, i) for i in range(n - 1)])  18.1 us
    ppermute x15, starting transfers between devices, reduce_pair(): return [lax.ppermute(parts[d], 'pair', ring(GROUPS, d)) for d in (1, 2, 3)]  17.7 us
    ppermute x5, starting transfers between devices, from_neighbours(): low = lax.ppermute(x, 'sec', [(i, i + 1) for i in range(n - 1)])  11.2 us
    pallas_call x1, Pallas kernels, on_device(): call(lambda *refs: start_kernel(count, *refs), 'start', [SM] * 3 + [VM] *...  6.34 us
    pallas_call x1, Pallas kernels, on_device(): call(first_kernel, 'first', [SM] * 3 + [VM] * 6, [BLOCK3, BLOCK3] + parts...  6.04 us
  transfers between devices with their start and end apart: 25, of which 14 were waited for; matrix products, arithmetic and copies ran while one was open for 0% of the time, Pallas kernels for 0%

profile of v1, /device:TPU:1, one launch (start us, length us, event | category | flops | bytes accessed | tf_op | source)
XLA Modules:
  0.0 267.9 jit_solution(12738347332355030416)
XLA Ops:
  4.5 5.1 %collective-permute-start.1 = (f32[520,128]{1,0:T(8,128)S(1)}, f32[520,128]{1,0:T(8,128)S(1)}, u32[]{:S(2)}, u32[]{:S(2)}) collective-permute-start(f32[520,128]{1,0:T(8,128)S(1)} %pack.1), channel_id=1, source_target_pairs={{4,0},{8,4},{12,8},{16,12},{20,16},{24,20},{28,24},{32,28},{36,32}... | collective-permute-start | bytes 798728 | tf_op jit(solution)/shard_map/ppermute | solution.py:257
  9.7 1.9 collective-permute-start
  16.1 6.0 %first.1 = (f32[3,4,128,128]{3,2,1,0:T(8,128)S(1)}, f32[3,4,128,128]{3,2,1,0:T(8,128)S(1)}, f32[4,128,128]{2,1,0:T(8,128)S(1)}, f32[4,128,128]{2,1,0:T(8,128)S(1...) custom-call(s32[1]{0:T(128)} %bitcast.group.refs_0_, s32[6]{0:T(128)S(1)} %copy-done.13, ...), custom_call_target="tpu_custom_call" | custom-call | tf_op jit(solution)/shard_map/first/pallas_call | solution.py:288
  22.9 2.6 collective-permute-start.3
  26.6 4.2 %collective-permute-done.2.r1 = f32[4,128,128]{2,1,0:T(8,128)S(1)} collective-permute-done((f32[4,128,128]{2,1,0:T(8,128)S(1)}, f32[4,128,128]{2,1,0:T(8,128)S(1)}, u32[]{:S(2)}, u32[]{:S(2)}) %collective-permute-start.2) | collective-permute-done | bytes 262176 | tf_op jit(solution)/shard_map/ppermute | solution.py:251
  30.8 6.9 %collective-permute-done.3.r2 = f32[4,128,128]{2,1,0:T(8,128)S(1)} collective-permute-done((f32[4,128,128]{2,1,0:T(8,128)S(1)}, f32[4,128,128]{2,1,0:T(8,128)S(1)}, u32[]{:S(2)}, u32[]{:S(2)}) %collective-permute-start.3) | collective-permute-done | bytes 262176 | tf_op jit(solution)/shard_map/ppermute | solution.py:251
  37.9 2.6 collective-permute-start.6
  40.5 3.0 %collective-permute-start.5 = (f32[4,128,128]{2,1,0:T(8,128)S(1)}, f32[4,128,128]{2,1,0:T(8,128)S(1)}, u32[]{:S(2)}, u32[]{:S(2)}) collective-permute-start(f32[4,128,128]{2,1,0:T(8,128)S(1)} %get-tuple-element.62.refs_6_.refs_9_), channel_id=1, source_target_pairs={{0,4},{4,8},{8,12},{12,16},{16,20},{20,24},{24,28},{28,32},{32,36}... | collective-permute-start | bytes 786440 | tf_op jit(solution)/shard_map/ppermute | solution.py:256
  43.5 29.2 %all_to_all.25 = f32[256,1,128]{2,1,0:T(1,128)S(1)} all-to-all(f32[256,1,128]{2,1,0:T(1,128)S(1)} %bitcast.36), channel_id=1, replica_groups=mesh['sec'=64,'pair'=4] {'sec','pair'}, dimensions={0} | all-to-all | bytes 262144 | tf_op jit(solution)/shard_map/all_to_all | solution.py:262
  72.7 6.3 %start.1 = (f32[3,4,128,128]{3,2,1,0:T(8,128)S(1)}, f32[8,128]{1,0:T(8,128)S(1)}, f32[4,128,128]{2,1,0:T(8,128)S(1)}, f32[4,128,128]{2,1,0:T(8,128)S(1)}, f32[4,...) custom-call(s32[1]{0:T(128)} %bitcast.group.refs_0_, s32[6]{0:T(128)S(1)} %copy-done.13, ...), custom_call_target="tpu_custom_call" | custom-call | tf_op jit(solution)/shard_map/start/pallas_call | solution.py:298
  79.5 1.8 collective-permute-start.8
  82.4 5.4 %collective-permute-done.7.r1 = f32[4,128,128]{2,1,0:T(8,128)S(1)} collective-permute-done((f32[4,128,128]{2,1,0:T(8,128)S(1)}, f32[4,128,128]{2,1,0:T(8,128)S(1)}, u32[]{:S(2)}, u32[]{:S(2)}) %collective-permute-start.7) | collective-permute-done | bytes 262176 | tf_op jit(solution)/shard_map/ppermute | solution.py:251
  87.8 5.1 %collective-permute-done.8.r2 = f32[4,128,128]{2,1,0:T(8,128)S(1)} collective-permute-done((f32[4,128,128]{2,1,0:T(8,128)S(1)}, f32[4,128,128]{2,1,0:T(8,128)S(1)}, u32[]{:S(2)}, u32[]{:S(2)}) %collective-permute-start.8) | collective-permute-done | bytes 262176 | tf_op jit(solution)/shard_map/ppermute | solution.py:251
  94.1 3.5 %collective-permute-start.11 = (f32[4,128,128]{2,1,0:T(8,128)S(1)}, f32[4,128,128]{2,1,0:T(8,128)S(1)}, u32[]{:S(2)}, u32[]{:S(2)}) collective-permute-start(f32[4,128,128]{2,1,0:T(8,128)S(1)} %get-tuple-element.70.refs_12_), channel_id=1, source_target_pairs={{4,0},{8,4},{12,8},{16,12},{20,16},{24,20},{28,24},{32,28},{36,32}... | collective-permute-start | bytes 786440 | tf_op jit(solution)/shard_map/ppermute | solution.py:257
  97.6 2.1 collective-permute-start.10
  99.7 22.7 %all_to_all.26 = f32[256,1,128]{2,1,0:T(1,128)S(1)} all-to-all(f32[256,1,128]{2,1,0:T(1,128)S(1)} %bitcast.37), channel_id=1, replica_groups=mesh['sec'=64,'pair'=4] {'sec','pair'}, dimensions={0} | all-to-all | bytes 262144 | tf_op jit(solution)/shard_map/all_to_all | solution.py:262
  122.3 7.3 %next.3 = (f32[3,4,128,128]{3,2,1,0:T(8,128)S(1)}, f32[3,4,128,128]{3,2,1,0:T(8,128)S(1)}, f32[3,4,128,128]{3,2,1,0:T(8,128)S(1)}, f32[8,128]{1,0:T(8,128)S(1)},...) custom-call(s32[1]{0:T(128)} %bitcast.group.refs_0_, ...), custom_call_target="tpu_custom_call" | custom-call | tf_op jit(solution)/shard_map/next/pallas_call | solution.py:318
  133.0 5.4 %collective-permute-done.12.r1 = f32[4,128,128]{2,1,0:T(8,128)S(1)} collective-permute-done((f32[4,128,128]{2,1,0:T(8,128)S(1)}, f32[4,128,128]{2,1,0:T(8,128)S(1)}, u32[]{:S(2)}, u32[]{:S(2)}) %collective-permute-start.12) | collective-permute-done | bytes 262176 | tf_op jit(solution)/shard_map/ppermute | solution.py:251
  138.3 5.1 %collective-permute-done.13.r2 = f32[4,128,128]{2,1,0:T(8,128)S(1)} collective-permute-done((f32[4,128,128]{2,1,0:T(8,128)S(1)}, f32[4,128,128]{2,1,0:T(8,128)S(1)}, u32[]{:S(2)}, u32[]{:S(2)}) %collective-permute-start.13) | collective-permute-done | bytes 262176 | tf_op jit(solution)/shard_map/ppermute | solution.py:251
  144.7 3.5 %collective-permute-start.16 = (f32[4,128,128]{2,1,0:T(8,128)S(1)}, f32[4,128,128]{2,1,0:T(8,128)S(1)}, u32[]{:S(2)}, u32[]{:S(2)}) collective-permute-start(f32[4,128,128]{2,1,0:T(8,128)S(1)} %get-tuple-element.80.refs_12_), channel_id=1, source_target_pairs={{4,0},{8,4},{12,8},{16,12},{20,16},{24,20},{28,24},{32,28},{36,32}... | collective-permute-start | bytes 786440 | tf_op jit(solution)/shard_map/ppermute | solution.py:257
  148.1 2.1 collective-permute-start.15
  150.2 22.7 %all_to_all.27 = f32[256,1,128]{2,1,0:T(1,128)S(1)} all-to-all(f32[256,1,128]{2,1,0:T(1,128)S(1)} %bitcast.38), channel_id=1, replica_groups=mesh['sec'=64,'pair'=4] {'sec','pair'}, dimensions={0} | all-to-all | bytes 262144 | tf_op jit(solution)/shard_map/all_to_all | solution.py:262
  172.9 7.3 %next.4 = (f32[3,4,128,128]{3,2,1,0:T(8,128)S(1)}, f32[3,4,128,128]{3,2,1,0:T(8,128)S(1)}, f32[3,4,128,128]{3,2,1,0:T(8,128)S(1)}, f32[8,128]{1,0:T(8,128)S(1)},...) custom-call(s32[1]{0:T(128)} %bitcast.group.refs_0_, ...), custom_call_target="tpu_custom_call" | custom-call | tf_op jit(solution)/shard_map/next/pallas_call | solution.py:318
  183.6 5.4 %collective-permute-done.17.r1 = f32[4,128,128]{2,1,0:T(8,128)S(1)} collective-permute-done((f32[4,128,128]{2,1,0:T(8,128)S(1)}, f32[4,128,128]{2,1,0:T(8,128)S(1)}, u32[]{:S(2)}, u32[]{:S(2)}) %collective-permute-start.17) | collective-permute-done | bytes 262176 | tf_op jit(solution)/shard_map/ppermute | solution.py:251
  188.9 5.1 %collective-permute-done.18.r2 = f32[4,128,128]{2,1,0:T(8,128)S(1)} collective-permute-done((f32[4,128,128]{2,1,0:T(8,128)S(1)}, f32[4,128,128]{2,1,0:T(8,128)S(1)}, u32[]{:S(2)}, u32[]{:S(2)}) %collective-permute-start.18) | collective-permute-done | bytes 262176 | tf_op jit(solution)/shard_map/ppermute | solution.py:251
  195.3 3.5 %collective-permute-start.21 = (f32[4,128,128]{2,1,0:T(8,128)S(1)}, f32[4,128,128]{2,1,0:T(8,128)S(1)}, u32[]{:S(2)}, u32[]{:S(2)}) collective-permute-start(f32[4,128,128]{2,1,0:T(8,128)S(1)} %get-tuple-element.90.refs_12_), channel_id=1, source_target_pairs={{4,0},{8,4},{12,8},{16,12},{20,16},{24,20},{28,24},{32,28},{36,32}... | collective-permute-start | bytes 786440 | tf_op jit(solution)/shard_map/ppermute | solution.py:257
  198.7 2.1 collective-permute-start.20
  200.8 22.7 %all_to_all.28 = f32[256,1,128]{2,1,0:T(1,128)S(1)} all-to-all(f32[256,1,128]{2,1,0:T(1,128)S(1)} %bitcast.39), channel_id=1, replica_groups=mesh['sec'=64,'pair'=4] {'sec','pair'}, dimensions={0} | all-to-all | bytes 262144 | tf_op jit(solution)/shard_map/all_to_all | solution.py:262
  223.5 7.3 %next.5 = (f32[3,4,128,128]{3,2,1,0:T(8,128)S(1)}, f32[3,4,128,128]{3,2,1,0:T(8,128)S(1)}, f32[3,4,128,128]{3,2,1,0:T(8,128)S(1)}, f32[8,128]{1,0:T(8,128)S(1)},...) custom-call(s32[1]{0:T(128)} %bitcast.group.refs_0_, ...), custom_call_target="tpu_custom_call" | custom-call | tf_op jit(solution)/shard_map/next/pallas_call | solution.py:318
  234.2 5.4 %collective-permute-done.22.r1 = f32[4,128,128]{2,1,0:T(8,128)S(1)} collective-permute-done((f32[4,128,128]{2,1,0:T(8,128)S(1)}, f32[4,128,128]{2,1,0:T(8,128)S(1)}, u32[]{:S(2)}, u32[]{:S(2)}) %collective-permute-start.22) | collective-permute-done | bytes 262176 | tf_op jit(solution)/shard_map/ppermute | solution.py:251
  239.5 5.1 %collective-permute-done.23.r2 = f32[4,128,128]{2,1,0:T(8,128)S(1)} collective-permute-done((f32[4,128,128]{2,1,0:T(8,128)S(1)}, f32[4,128,128]{2,1,0:T(8,128)S(1)}, u32[]{:S(2)}, u32[]{:S(2)}) %collective-permute-start.23) | collective-permute-done | bytes 262176 | tf_op jit(solution)/shard_map/ppermute | solution.py:251
  246.4 20.1 %all_to_all.29 = f32[256,1,128]{2,1,0:T(1,128)S(1)} all-to-all(f32[256,1,128]{2,1,0:T(1,128)S(1)} %bitcast.40), channel_id=1, replica_groups=mesh['sec'=64,'pair'=4] {'sec','pair'}, dimensions={0} | all-to-all | bytes 262144 | tf_op jit(solution)/shard_map/all_to_all | solution.py:262
  (67 shorter events, 27.8 us)
Async XLA Ops:
  0.6 15.5 %copy-start.13 = (s32[6]{0:T(128)S(1)}, s32[6]{0:T(128)}, u32[]{:S(2)}) copy-start(s32[6]{0:T(128)} %refs_1_.7) | copy-start | bytes 76
  4.5 11.6 %collective-permute-start.1 = (f32[520,128]{1,0:T(8,128)S(1)}, f32[520,128]{1,0:T(8,128)S(1)}, u32[]{:S(2)}, u32[]{:S(2)}) collective-permute-start(f32[520,128]{1,0:T(8,128)S(1)} %pack.1), channel_id=1, source_target_pairs={{4,0},{8,4},{12,8},{16,12},{20,16},{24,20},{28,24},{32,28},{36,32}... | collective-permute-start | bytes 798728 | tf_op jit(solution)/shard_map/ppermute | solution.py:257
  9.7 6.4 %collective-permute-start = (f32[520,128]{1,0:T(8,128)S(1)}, f32[520,128]{1,0:T(8,128)S(1)}, u32[]{:S(2)}, u32[]{:S(2)}) collective-permute-start(f32[520,128]{1,0:T(8,128)S(1)} %pack.1), channel_id=1, source_target_pairs={{0,4},{4,8},{8,12},{12,16},{16,20},{20,24},{24,28},{28,32},{32,36}... | collective-permute-start | bytes 798728 | tf_op jit(solution)/shard_map/ppermute | solution.py:256
  16.1 21.9 %copy-start = (bf16[6,4,128,256]{3,2,1,0:T(8,128)(2,1)}, bf16[6,4,128,256]{3,2,1,0:T(8,128)(2,1)S(1)}, u32[]{:S(2)}) copy-start(bf16[6,4,128,256]{3,2,1,0:T(8,128)(2,1)S(1)} %get-tuple-element.53.right2.refs_10_.refs_15_) | copy-start | bytes 4718596
  22.1 56.9 %copy-start.1 = (f32[3,4,128,128]{3,2,1,0:T(8,128)}, f32[3,4,128,128]{3,2,1,0:T(8,128)S(1)}, u32[]{:S(2)}) copy-start(f32[3,4,128,128]{3,2,1,0:T(8,128)S(1)} %get-tuple-element.61.refs_5_.refs_6_) | copy-start | bytes 2359300
  22.2 71.6 %copy-start.4 = (f32[3,4,128,128]{3,2,1,0:T(8,128)}, f32[3,4,128,128]{3,2,1,0:T(8,128)S(1)}, u32[]{:S(2)}) copy-start(f32[3,4,128,128]{3,2,1,0:T(8,128)S(1)} %get-tuple-element.59.state.refs_4_.refs_5_) | copy-start | bytes 2359300
  22.2 8.6 %collective-permute-start.2 = (f32[4,128,128]{2,1,0:T(8,128)S(1)}, f32[4,128,128]{2,1,0:T(8,128)S(1)}, u32[]{:S(2)}, u32[]{:S(2)}) collective-permute-start(f32[4,128,128]{2,1,0:T(8,128)S(1)} %get-tuple-element.56), channel_id=1, source_target_pairs={{0,1},{1,2},{2,3},{3,0},{4,5},{5,6},{6,7},{7,4},{8,9},{9,10},{10,1... | collective-permute-start | bytes 786440 | tf_op jit(solution)/shard_map/ppermute | solution.py:251
  22.9 14.8 %collective-permute-start.3 = (f32[4,128,128]{2,1,0:T(8,128)S(1)}, f32[4,128,128]{2,1,0:T(8,128)S(1)}, u32[]{:S(2)}, u32[]{:S(2)}) collective-permute-start(f32[4,128,128]{2,1,0:T(8,128)S(1)} %get-tuple-element.57), channel_id=1, source_target_pairs={{0,2},{1,3},{2,0},{3,1},{4,6},{5,7},{6,4},{7,5},{8,10},{9,11},{10,... | collective-permute-start | bytes 786440 | tf_op jit(solution)/shard_map/ppermute | solution.py:251
  25.5 12.2 %collective-permute-start.4 = (f32[4,128,128]{2,1,0:T(8,128)S(1)}, f32[4,128,128]{2,1,0:T(8,128)S(1)}, u32[]{:S(2)}, u32[]{:S(2)}) collective-permute-start(f32[4,128,128]{2,1,0:T(8,128)S(1)} %get-tuple-element.58), channel_id=1, source_target_pairs={{0,3},{1,0},{2,1},{3,2},{4,7},{5,4},{6,5},{7,6},{8,11},{9,8},{10,9... | collective-permute-start | bytes 786440 | tf_op jit(solution)/shard_map/ppermute | solution.py:251
  37.9 34.8 %collective-permute-start.6 = (f32[4,128,128]{2,1,0:T(8,128)S(1)}, f32[4,128,128]{2,1,0:T(8,128)S(1)}, u32[]{:S(2)}, u32[]{:S(2)}) collective-permute-start(f32[4,128,128]{2,1,0:T(8,128)S(1)} %get-tuple-element.62.refs_6_.refs_9_), channel_id=1, source_target_pairs={{4,0},{8,4},{12,8},{16,12},{20,16},{24,20},{28,24},{32,28},{36,32}... | collective-permute-start | bytes 786440 | tf_op jit(solution)/shard_map/ppermute | solution.py:257
  40.5 32.2 %collective-permute-start.5 = (f32[4,128,128]{2,1,0:T(8,128)S(1)}, f32[4,128,128]{2,1,0:T(8,128)S(1)}, u32[]{:S(2)}, u32[]{:S(2)}) collective-permute-start(f32[4,128,128]{2,1,0:T(8,128)S(1)} %get-tuple-element.62.refs_6_.refs_9_), channel_id=1, source_target_pairs={{0,4},{4,8},{8,12},{12,16},{16,20},{20,24},{24,28},{28,32},{32,36}... | collective-permute-start | bytes 786440 | tf_op jit(solution)/shard_map/ppermute | solution.py:256
  79.1 43.2 %copy-start.7 = (f32[3,4,128,128]{3,2,1,0:T(8,128)}, f32[3,4,128,128]{3,2,1,0:T(8,128)S(1)}, u32[]{:S(2)}) copy-start(f32[3,4,128,128]{3,2,1,0:T(8,128)S(1)} %get-tuple-element.67.corr.refs_7_) | copy-start | bytes 2359300
  79.1 8.7 %collective-permute-start.7 = (f32[4,128,128]{2,1,0:T(8,128)S(1)}, f32[4,128,128]{2,1,0:T(8,128)S(1)}, u32[]{:S(2)}, u32[]{:S(2)}) collective-permute-start(f32[4,128,128]{2,1,0:T(8,128)S(1)} %get-tuple-element.64), channel_id=1, source_target_pairs={{0,1},{1,2},{2,3},{3,0},{4,5},{5,6},{6,7},{7,4},{8,9},{9,10},{10,1... | collective-permute-start | bytes 786440 | tf_op jit(solution)/shard_map/ppermute | solution.py:251
  79.5 13.4 %collective-permute-start.8 = (f32[4,128,128]{2,1,0:T(8,128)S(1)}, f32[4,128,128]{2,1,0:T(8,128)S(1)}, u32[]{:S(2)}, u32[]{:S(2)}) collective-permute-start(f32[4,128,128]{2,1,0:T(8,128)S(1)} %get-tuple-element.65), channel_id=1, source_target_pairs={{0,2},{1,3},{2,0},{3,1},{4,6},{5,7},{6,4},{7,5},{8,10},{9,11},{10,... | collective-permute-start | bytes 786440 | tf_op jit(solution)/shard_map/ppermute | solution.py:251
  81.4 12.4 %collective-permute-start.9 = (f32[4,128,128]{2,1,0:T(8,128)S(1)}, f32[4,128,128]{2,1,0:T(8,128)S(1)}, u32[]{:S(2)}, u32[]{:S(2)}) collective-permute-start(f32[4,128,128]{2,1,0:T(8,128)S(1)} %get-tuple-element.66), channel_id=1, source_target_pairs={{0,3},{1,0},{2,1},{3,2},{4,7},{5,4},{6,5},{7,6},{8,11},{9,8},{10,9... | collective-permute-start | bytes 786440 | tf_op jit(solution)/shard_map/ppermute | solution.py:251
  94.1 28.2 %collective-permute-start.11 = (f32[4,128,128]{2,1,0:T(8,128)S(1)}, f32[4,128,128]{2,1,0:T(8,128)S(1)}, u32[]{:S(2)}, u32[]{:S(2)}) collective-permute-start(f32[4,128,128]{2,1,0:T(8,128)S(1)} %get-tuple-element.70.refs_12_), channel_id=1, source_target_pairs={{4,0},{8,4},{12,8},{16,12},{20,16},{24,20},{28,24},{32,28},{36,32}... | collective-permute-start | bytes 786440 | tf_op jit(solution)/shard_map/ppermute | solution.py:257
  97.6 24.8 %collective-permute-start.10 = (f32[4,128,128]{2,1,0:T(8,128)S(1)}, f32[4,128,128]{2,1,0:T(8,128)S(1)}, u32[]{:S(2)}, u32[]{:S(2)}) collective-permute-start(f32[4,128,128]{2,1,0:T(8,128)S(1)} %get-tuple-element.70.refs_12_), channel_id=1, source_target_pairs={{0,4},{4,8},{8,12},{12,16},{16,20},{20,24},{24,28},{28,32},{32,36}... | collective-permute-start | bytes 786440 | tf_op jit(solution)/shard_map/ppermute | solution.py:256
  129.6 15.0 %copy-start.3 = (f32[3,4,128,128]{3,2,1,0:T(8,128)}, f32[3,4,128,128]{3,2,1,0:T(8,128)S(1)}, u32[]{:S(2)}) copy-start(f32[3,4,128,128]{3,2,1,0:T(8,128)S(1)} %get-tuple-element.77.image.refs_8_.refs_9_.refs_10_) | copy-start | bytes 2359300
  129.6 15.0 %copy-start.6 = (f32[3,4,128,128]{3,2,1,0:T(8,128)}, f32[3,4,128,128]{3,2,1,0:T(8,128)S(1)}, u32[]{:S(2)}) copy-start(f32[3,4,128,128]{3,2,1,0:T(8,128)S(1)} %get-tuple-element.76.corr.refs_7_) | copy-start | bytes 2359300
  129.7 8.7 %collective-permute-start.12 = (f32[4,128,128]{2,1,0:T(8,128)S(1)}, f32[4,128,128]{2,1,0:T(8,128)S(1)}, u32[]{:S(2)}, u32[]{:S(2)}) collective-permute-start(f32[4,128,128]{2,1,0:T(8,128)S(1)} %get-tuple-element.72), channel_id=1, source_target_pairs={{0,1},{1,2},{2,3},{3,0},{4,5},{5,6},{6,7},{7,4},{8,9},{9,10},{10,1... | collective-permute-start | bytes 786440 | tf_op jit(solution)/shard_map/ppermute | solution.py:251
  130.1 13.3 %collective-permute-start.13 = (f32[4,128,128]{2,1,0:T(8,128)S(1)}, f32[4,128,128]{2,1,0:T(8,128)S(1)}, u32[]{:S(2)}, u32[]{:S(2)}) collective-permute-start(f32[4,128,128]{2,1,0:T(8,128)S(1)} %get-tuple-element.73), channel_id=1, source_target_pairs={{0,2},{1,3},{2,0},{3,1},{4,6},{5,7},{6,4},{7,5},{8,10},{9,11},{10,... | collective-permute-start | bytes 786440 | tf_op jit(solution)/shard_map/ppermute | solution.py:251
  131.9 12.4 %collective-permute-start.14 = (f32[4,128,128]{2,1,0:T(8,128)S(1)}, f32[4,128,128]{2,1,0:T(8,128)S(1)}, u32[]{:S(2)}, u32[]{:S(2)}) collective-permute-start(f32[4,128,128]{2,1,0:T(8,128)S(1)} %get-tuple-element.74), channel_id=1, source_target_pairs={{0,3},{1,0},{2,1},{3,2},{4,7},{5,4},{6,5},{7,6},{8,11},{9,8},{10,9... | collective-permute-start | bytes 786440 | tf_op jit(solution)/shard_map/ppermute | solution.py:251
  144.7 28.2 %collective-permute-start.16 = (f32[4,128,128]{2,1,0:T(8,128)S(1)}, f32[4,128,128]{2,1,0:T(8,128)S(1)}, u32[]{:S(2)}, u32[]{:S(2)}) collective-permute-start(f32[4,128,128]{2,1,0:T(8,128)S(1)} %get-tuple-element.80.refs_12_), channel_id=1, source_target_pairs={{4,0},{8,4},{12,8},{16,12},{20,16},{24,20},{28,24},{32,28},{36,32}... | collective-permute-start | bytes 786440 | tf_op jit(solution)/shard_map/ppermute | solution.py:257
  148.1 24.8 %collective-permute-start.15 = (f32[4,128,128]{2,1,0:T(8,128)S(1)}, f32[4,128,128]{2,1,0:T(8,128)S(1)}, u32[]{:S(2)}, u32[]{:S(2)}) collective-permute-start(f32[4,128,128]{2,1,0:T(8,128)S(1)} %get-tuple-element.80.refs_12_), channel_id=1, source_target_pairs={{0,4},{4,8},{8,12},{12,16},{16,20},{20,24},{24,28},{28,32},{32,36}... | collective-permute-start | bytes 786440 | tf_op jit(solution)/shard_map/ppermute | solution.py:256
  180.3 8.7 %collective-permute-start.17 = (f32[4,128,128]{2,1,0:T(8,128)S(1)}, f32[4,128,128]{2,1,0:T(8,128)S(1)}, u32[]{:S(2)}, u32[]{:S(2)}) collective-permute-start(f32[4,128,128]{2,1,0:T(8,128)S(1)} %get-tuple-element.82), channel_id=1, source_target_pairs={{0,1},{1,2},{2,3},{3,0},{4,5},{5,6},{6,7},{7,4},{8,9},{9,10},{10,1... | collective-permute-start | bytes 786440 | tf_op jit(solution)/shard_map/ppermute | solution.py:251
  180.7 13.4 %collective-permute-start.18 = (f32[4,128,128]{2,1,0:T(8,128)S(1)}, f32[4,128,128]{2,1,0:T(8,128)S(1)}, u32[]{:S(2)}, u32[]{:S(2)}) collective-permute-start(f32[4,128,128]{2,1,0:T(8,128)S(1)} %get-tuple-element.83), channel_id=1, source_target_pairs={{0,2},{1,3},{2,0},{3,1},{4,6},{5,7},{6,4},{7,5},{8,10},{9,11},{10,... | collective-permute-start | bytes 786440 | tf_op jit(solution)/shard_map/ppermute | solution.py:251
  182.5 12.4 %collective-permute-start.19 = (f32[4,128,128]{2,1,0:T(8,128)S(1)}, f32[4,128,128]{2,1,0:T(8,128)S(1)}, u32[]{:S(2)}, u32[]{:S(2)}) collective-permute-start(f32[4,128,128]{2,1,0:T(8,128)S(1)} %get-tuple-element.84), channel_id=1, source_target_pairs={{0,3},{1,0},{2,1},{3,2},{4,7},{5,4},{6,5},{7,6},{8,11},{9,8},{10,9... | collective-permute-start | bytes 786440 | tf_op jit(solution)/shard_map/ppermute | solution.py:251
  195.3 28.2 %collective-permute-start.21 = (f32[4,128,128]{2,1,0:T(8,128)S(1)}, f32[4,128,128]{2,1,0:T(8,128)S(1)}, u32[]{:S(2)}, u32[]{:S(2)}) collective-permute-start(f32[4,128,128]{2,1,0:T(8,128)S(1)} %get-tuple-element.90.refs_12_), channel_id=1, source_target_pairs={{4,0},{8,4},{12,8},{16,12},{20,16},{24,20},{28,24},{32,28},{36,32}... | collective-permute-start | bytes 786440 | tf_op jit(solution)/shard_map/ppermute | solution.py:257
  198.7 24.8 %collective-permute-start.20 = (f32[4,128,128]{2,1,0:T(8,128)S(1)}, f32[4,128,128]{2,1,0:T(8,128)S(1)}, u32[]{:S(2)}, u32[]{:S(2)}) collective-permute-start(f32[4,128,128]{2,1,0:T(8,128)S(1)} %get-tuple-element.90.refs_12_), channel_id=1, source_target_pairs={{0,4},{4,8},{8,12},{12,16},{16,20},{20,24},{24,28},{28,32},{32,36}... | collective-permute-start | bytes 786440 | tf_op jit(solution)/shard_map/ppermute | solution.py:256
  230.9 8.7 %collective-permute-start.22 = (f32[4,128,128]{2,1,0:T(8,128)S(1)}, f32[4,128,128]{2,1,0:T(8,128)S(1)}, u32[]{:S(2)}, u32[]{:S(2)}) collective-permute-start(f32[4,128,128]{2,1,0:T(8,128)S(1)} %get-tuple-element.92), channel_id=1, source_target_pairs={{0,1},{1,2},{2,3},{3,0},{4,5},{5,6},{6,7},{7,4},{8,9},{9,10},{10,1... | collective-permute-start | bytes 786440 | tf_op jit(solution)/shard_map/ppermute | solution.py:251
  231.3 13.4 %collective-permute-start.23 = (f32[4,128,128]{2,1,0:T(8,128)S(1)}, f32[4,128,128]{2,1,0:T(8,128)S(1)}, u32[]{:S(2)}, u32[]{:S(2)}) collective-permute-start(f32[4,128,128]{2,1,0:T(8,128)S(1)} %get-tuple-element.93), channel_id=1, source_target_pairs={{0,2},{1,3},{2,0},{3,1},{4,6},{5,7},{6,4},{7,5},{8,10},{9,11},{10,... | collective-permute-start | bytes 786440 | tf_op jit(solution)/shard_map/ppermute | solution.py:251
  233.1 12.4 %collective-permute-start.24 = (f32[4,128,128]{2,1,0:T(8,128)S(1)}, f32[4,128,128]{2,1,0:T(8,128)S(1)}, u32[]{:S(2)}, u32[]{:S(2)}) collective-permute-start(f32[4,128,128]{2,1,0:T(8,128)S(1)} %get-tuple-element.94), channel_id=1, source_target_pairs={{0,3},{1,0},{2,1},{3,2},{4,7},{5,4},{6,5},{7,6},{8,11},{9,8},{10,9... | collective-permute-start | bytes 786440 | tf_op jit(solution)/shard_map/ppermute | solution.py:251
  (7 other events, 35.0 us)

commit v2 on v1

v2 whole, which is shorter than its diff:
```python
import jax
import jax.numpy as jnp
from jax import lax
from jax.experimental import pallas as pl
from jax.experimental.pallas import tpu as pltpu
from jax.sharding import PartitionSpec as P

ITERS = 4
TERMS = 6
LOCAL = 4
GROUPS = 4
B = 128

f32 = jnp.float32
bf16 = jnp.bfloat16
VM = pl.BlockSpec(memory_space=pltpu.VMEM)
SM = pl.BlockSpec(memory_space=pltpu.SMEM)
PARAMS = pltpu.CompilerParams(vmem_limit_bytes=48 * 1024 * 1024)


def halves(x):
    high = x.astype(bf16)
    return high, (x - high.astype(f32)).astype(bf16)


def eye_mask():
    return lax.broadcasted_iota(jnp.int32, (B, B), 0) == lax.broadcasted_iota(jnp.int32, (B, B), 1)


def row_mask(rows):
    return (lax.broadcasted_iota(jnp.int32, (B, B), 0) < rows[0]).astype(f32)


def mask_kernel(rows, psi, state):
    keep = row_mask(rows)
    for p in range(LOCAL):
        state[p] = psi[p] * keep


def split_kernel(group, shift, rows, weights, left, right, left2, right2, diag):
    keep = row_mask(rows)
    eye = eye_mask()
    left_lines = []
    for k in range(TERMS):
        block = left[k] * keep
        left2[k] = jnp.concatenate(halves(block), axis=1)
        chosen = jnp.where(shift[k] == 0, 1.0, 0.0).astype(f32)
        left_lines.append(jnp.sum(jnp.where(eye, block, 0.0), axis=0, keepdims=True) * chosen)
    pad = jnp.zeros((8 - TERMS, B), f32)
    left_lines = jnp.concatenate(left_lines + [pad], axis=0)
    for q in range(LOCAL):
        lines = []
        for k in range(TERMS):
            block = right[k, q]
            right2[k, q] = jnp.concatenate(halves(jnp.transpose(block)), axis=1)
            p = group[0] * LOCAL + q
            scale = weights[k * 256 + p * 16 + p]
            lines.append(jnp.sum(jnp.where(eye, block, 0.0), axis=0, keepdims=True) * scale)
        diag[q] = lax.dot_general(
            left_lines, jnp.concatenate(lines + [pad], axis=0), (((0,), (0,)), ((), ())),
            precision=lax.Precision.HIGHEST, preferred_element_type=f32)


def mix(group, weights, z, out, target):
    for half in range(2):
        first = target * LOCAL + 2 * half
        acc = [None, None]
        for k in range(TERMS):
            for q in range(LOCAL):
                block = z[k * LOCAL + q]
                for j in range(2):
                    at = k * 256 + (first + j) * 16 + group[0] * LOCAL + q
                    part = weights[at] * block
                    acc[j] = part if acc[j] is None else acc[j] + part
        for j in range(2):
            out[2 * half + j] = acc[j]


def terms_kernel(group, sector, shift, weights, own, by_chip, by_core, left2, right2, z, out, vec2):
    odd = lax.rem(sector[0], 2)
    for p in range(LOCAL):
        vec2[1, p] = jnp.concatenate(halves(own[p]), axis=1)
        vec2[2 - 2 * odd, p] = jnp.concatenate(halves(by_core[p]), axis=1)
        vec2[2 * odd, p] = jnp.concatenate(halves(by_chip[p]), axis=1)
    for k in range(TERMS):
        source = shift[k] + 1
        lhs = left2[k]
        for q in range(LOCAL):
            r = right2[k, q]
            x = jnp.dot(vec2[source, q], jnp.concatenate([r, r], axis=0), preferred_element_type=f32)
            xh, xl = halves(x[:, :B] + x[:, B:])
            both = jnp.concatenate([xh, xl], axis=1)
            y = jnp.dot(lhs, jnp.concatenate([both, both], axis=0), preferred_element_type=f32)
            z[k * LOCAL + q] = y[:, :B] + y[:, B:]
    mix(group, weights, z, out, group[0] ^ 2)


def near_kernel(group, weights, z, out1, out3):
    mix(group, weights, z, out1, group[0] ^ 1)
    mix(group, weights, z, out3, group[0] ^ 3)


def own_kernel(group, weights, z, out):
    mix(group, weights, z, out, group[0])


def lane(row, j):
    at = lax.broadcasted_iota(jnp.int32, row.shape, 1) == j
    return jnp.sum(jnp.where(at, row, 0.0), axis=1, keepdims=True)


def put_lanes(values):
    at = lax.broadcasted_iota(jnp.int32, (1, B), 1)
    row = jnp.zeros((1, B), f32)
    for j, v in enumerate(values):
        row = jnp.where(at == j, v, row)
    return row


def lowest_root(lead, middle, const):
    root = jnp.sqrt(middle * middle - 4.0 * lead * const)
    return jnp.where(middle > 0, (-middle - root) / (2.0 * lead), 2.0 * const / (root - middle))


def ritz(sums, rayleigh, length):
    s_ic, c_i, curvature, correlation, spread = sums
    cross = 0.5 * (s_ic + c_i)
    lead = length * spread - correlation * correlation
    middle = -(length * curvature + spread * rayleigh - 2.0 * correlation * cross)
    const = rayleigh * curvature - cross * cross
    lowest = lowest_root(lead, middle, const)
    keep = curvature - lowest * spread
    add = lowest * correlation - cross
    norm = keep * keep * length + 2.0 * keep * add * correlation + add * add * spread
    factor = 1.0 / jnp.sqrt(norm)
    keep, add = keep * factor, add * factor
    rayleigh = keep * keep * rayleigh + 2.0 * keep * add * cross + add * add * curvature
    length = keep * keep * length + 2.0 * keep * add * correlation + add * add * spread
    return lowest, keep, add, rayleigh, length


def totals(stats, count, n):
    row = jnp.sum(stats[...], axis=0, keepdims=True) * (1.0 / count)
    return [lane(row, j) for j in range(n)]


def correct(state, image, diag, theta):
    return (image - theta * state) / jnp.maximum(jnp.abs(diag - theta), 1.0)


def start_kernel(count, stats, state, image, diag, corr, carry):
    rayleigh, length = totals(stats, count, 2)
    theta = rayleigh / length
    for p in range(LOCAL):
        corr[p] = correct(state[p], image[p], diag[p], theta)
    carry[...] = jnp.broadcast_to(put_lanes([rayleigh, length]), (8, B))


def next_kernel(count, step, stats, carry_in, state, image, diag, corr, more, state_out, image_out, corr_out, carry):
    sums = totals(stats, count, 5)
    old = carry_in[0:1, :]
    lowest, keep, add, rayleigh, length = ritz(sums, lane(old, 0), lane(old, 1))
    theta = rayleigh / length
    for p in range(LOCAL):
        s = keep * state[p] + add * corr[p]
        i = keep * image[p] + add * more[p]
        state_out[p] = s
        image_out[p] = i
        corr_out[p] = correct(s, i, diag[p], theta)
    energies = [lane(old, 2 + j) for j in range(step)] + [lowest]
    carry[...] = jnp.broadcast_to(put_lanes([rayleigh, length] + energies), (8, B))


def last_kernel(count, stats, carry_in, state, corr, state_out, energies):
    sums = totals(stats, count, 5)
    old = carry_in[0:1, :]
    lowest, keep, add, _, _ = ritz(sums, lane(old, 0), lane(old, 1))
    for p in range(LOCAL):
        state_out[p] = keep * state[p] + add * corr[p]
    for j, v in enumerate([lane(old, 2 + j) for j in range(ITERS - 1)] + [lowest]):
        energies[j] = v[0, 0]


def sum_all(block):
    return jnp.sum(jnp.sum(block, axis=0, keepdims=True), axis=1, keepdims=True)


def first_stats_kernel(own, r1, r2, r3, state, image, stats):
    a, b = jnp.zeros((B, B), f32), jnp.zeros((B, B), f32)
    for p in range(LOCAL):
        i = (own[p] + r2[p]) + (r1[p] + r3[p])
        s = state[p]
        image[p] = i
        a = a + s * i
        b = b + s * s
    stats[...] = jnp.broadcast_to(put_lanes([sum_all(a), sum_all(b)]), stats.shape)


def stats_kernel(own, r1, r2, r3, state, corr, image, image_corr, stats):
    acc = [jnp.zeros((B, B), f32) for _ in range(5)]
    for p in range(LOCAL):
        ic = (own[p] + r2[p]) + (r1[p] + r3[p])
        s, c, i = state[p], corr[p], image[p]
        image_corr[p] = ic
        for j, v in enumerate((s * ic, c * i, c * ic, s * c, c * c)):
            acc[j] = acc[j] + v
    stats[...] = jnp.broadcast_to(put_lanes([sum_all(a) for a in acc]), stats.shape)


def arr(*shape, dtype=f32):
    return jax.ShapeDtypeStruct(shape, dtype)


BLOCK = arr(LOCAL, B, B)
TERM_BLOCKS = arr(TERMS * LOCAL, B, B)


def call(kernel, name, in_specs, outs, scratch=(), out_specs=None, flops=0):
    moved = sum(o.size * o.dtype.itemsize for o in outs)
    return pl.pallas_call(
        kernel,
        out_shape=outs,
        in_specs=in_specs,
        out_specs=out_specs or [VM] * len(outs),
        scratch_shapes=list(scratch),
        compiler_params=PARAMS,
        cost_estimate=pl.CostEstimate(flops=flops, bytes_accessed=2 * moved, transcendentals=0),
        name=name,
    )


def swap(x, step):
    return lax.ppermute(x, "pair", [(i, i ^ step) for i in range(GROUPS)])


def neighbours(x):
    n = lax.axis_size("sec")
    by_chip = lax.ppermute(x, "sec", [(i, i + 1 if i % 2 else i - 1) for i in range(1, n - 1)])
    by_core = lax.ppermute(x, "sec", [(i, i ^ 1) for i in range(n)])
    return by_chip, by_core


def exchange(stats, devices):
    got = lax.all_to_all(stats.reshape(devices, 1, B), ("sec", "pair"), 0, 0)
    return got.reshape(devices, B)


def on_device(psi_start, left_env, right_env, mpo_coef, mpo_pattern, sector_shift, block_rows):
    devices = lax.axis_size("sec") * lax.axis_size("pair")
    count = float(psi_start.size * devices)
    psi = psi_start.reshape(LOCAL, B, B)
    left = left_env.reshape(TERMS, B, B)
    group = lax.axis_index("pair").astype(jnp.int32).reshape(1)
    sector = lax.axis_index("sec").astype(jnp.int32).reshape(1)
    weights = (mpo_coef * mpo_pattern.astype(f32)).reshape(-1)
    stats_shape = arr(devices, B)
    carry_shape = arr(8, B)

    def shares(vector, near, left2, right2):
        by_chip, by_core = near
        z, part2 = call(
            terms_kernel, "terms", [SM] * 4 + [VM] * 5, [TERM_BLOCKS, BLOCK],
            [pltpu.VMEM((3, LOCAL, B, 2 * B), bf16)],
        )(group, sector, sector_shift, weights, vector, by_chip, by_core, left2, right2)
        got2 = swap(part2, 2)
        part1, part3 = call(near_kernel, "near", [SM, SM, VM], [BLOCK] * 2)(group, weights, z)
        got1, got3 = swap(part1, 1), swap(part3, 3)
        (own,) = call(own_kernel, "own", [SM, SM, VM], [BLOCK])(group, weights, z)
        return own, got1, got2, got3

    (state,) = call(mask_kernel, "mask", [SM, VM], [BLOCK])(block_rows, psi)
    near = neighbours(state)
    left2, right2, diag = call(
        split_kernel, "split", [SM] * 4 + [VM] * 2,
        [arr(TERMS, B, 2 * B, dtype=bf16), arr(TERMS, LOCAL, B, 2 * B, dtype=bf16), BLOCK],
    )(group, sector_shift, block_rows, weights, left, right_env)

    image, stats = call(first_stats_kernel, "first_stats", [VM] * 5, [BLOCK, stats_shape])(
        *shares(state, near, left2, right2), state)
    stats = exchange(stats, devices)
    corr, carry = call(
        lambda *refs: start_kernel(count, *refs), "start", [VM] * 4, [BLOCK, carry_shape]
    )(stats, state, image, diag)

    for step in range(ITERS):
        image_corr, stats = call(stats_kernel, "stats", [VM] * 7, [BLOCK, stats_shape])(
            *shares(corr, neighbours(corr), left2, right2), state, corr, image)
        stats = exchange(stats, devices)
        if step < ITERS - 1:
            state, image, corr, carry = call(
                lambda *refs, step=step: next_kernel(count, step, *refs), "next", [VM] * 7, [BLOCK] * 3 + [carry_shape]
            )(stats, carry, state, image, diag, corr, image_corr)

    state, energies = call(
        lambda *refs: last_kernel(count, *refs), "last", [VM] * 4, [BLOCK, arr(ITERS)], out_specs=[VM, SM]
    )(stats, carry, state, corr)
    return state.reshape(psi_start.shape), energies


def solution(mesh):
    in_specs = (
        P("sec", "pair", None, None),
        P(None, "sec", None, None),
        P(None, "pair", None, None),
        P(),
        P(),
        P(),
        P("sec"),
    )
    out_specs = (P("sec", "pair", None, None), P())
    return jax.shard_map(
        on_device, mesh=mesh, in_specs=in_specs, out_specs=out_specs, check_vma=False
    )
```

time: 269 us -> 243 us (0.903)
  starting transfers between devices: 47 us -> 33.8 us
  Pallas kernels: 38.9 us -> 27.4 us
  blocking collectives: 117 us -> 122 us
  waiting for transfers between devices: 56.7 us -> 52.2 us
    ppermute x25, starting transfers between devices: 47 us -> 33.8 us  [the longest x15 16.9 us: swap(): return lax.ppermute(x, 'pair', [(i, i ^ step) for i in range(GROUPS)])]
    pallas_call x13 -> x27, Pallas kernels: 38.9 us -> 27.4 us  [the longest x5 9.65 us: shares(): call(terms_kernel, 'terms', [SM] * 4 + [VM] * 5, [TERM_BLOCKS, BLOCK], [p...]
    all_to_all x5, blocking collectives: 117 us -> 122 us  [exchange(): got = lax.all_to_all(stats.reshape(devices, 1, B), ('sec', 'pair'), 0, 0)]
    ppermute x25, waiting for transfers between devices: 56.7 us -> 52.2 us  [the longest x15 29.5 us: swap(): return lax.ppermute(x, 'pair', [(i, i ^ step) for i in range(GROUPS)])]
  transfers between devices with their start and end apart: 25 -> 25, of which waited for: 14 -> 15; matrix products, arithmetic and copies ran while one was open for 0% -> 0% of each run, Pallas kernels for 0% -> 3%
where the time goes in v2:
time: 243 us; the launch traced here: 242 us
  blocking collectives  122 us (50%)
  waiting for transfers between devices  52.2 us (21%)
  starting transfers between devices  33.8 us (14%)
  Pallas kernels  27.4 us (11%)
  local copies, waits for them, and re-layouts  4.09 us (2%)
    all_to_all x5, blocking collectives, exchange(): got = lax.all_to_all(stats.reshape(devices, 1, B), ('sec', 'pair'), 0, 0)  122 us
    ppermute x15, waiting for transfers between devices, swap(): return lax.ppermute(x, 'pair', [(i, i ^ step) for i in range(GROUPS)])  29.5 us
    ppermute x5, waiting for transfers between devices, neighbours(): lax.ppermute(x, 'sec', [(i, i + 1 if i % 2 else i - 1) for i in range(1,...  22.7 us
    ppermute x15, starting transfers between devices, swap(): return lax.ppermute(x, 'pair', [(i, i ^ step) for i in range(GROUPS)])  16.9 us
    ppermute x5, starting transfers between devices, neighbours(): lax.ppermute(x, 'sec', [(i, i + 1 if i % 2 else i - 1) for i in range(1,...  10.4 us
    pallas_call x5, Pallas kernels, shares(): call(terms_kernel, 'terms', [SM] * 4 + [VM] * 5, [TERM_BLOCKS, BLOCK], [p...  9.65 us
    pallas_call x5, Pallas kernels, shares(): call(near_kernel, 'near', [SM, SM, VM], [BLOCK] * 2)(group, weights, z)  7.36 us
    ppermute x5, starting transfers between devices, neighbours(): by_core = lax.ppermute(x, 'sec', [(i, i ^ 1) for i in range(n)])  6.54 us
  transfers between devices with their start and end apart: 25, of which 15 were waited for; matrix products, arithmetic and copies ran while one was open for 0% of the time, Pallas kernels for 3%

profile of v2, /device:TPU:1, one launch (start us, length us, event | category | flops | bytes accessed | tf_op | source)
XLA Modules:
  0.0 242.5 jit_solution(4522996352135184711)
XLA Ops:
  2.3 3.3 %collective-permute-start.1 = (f32[4,128,128]{2,1,0:T(8,128)S(1)}, f32[4,128,128]{2,1,0:T(8,128)S(1)}, u32[]{:S(2)}, u32[]{:S(2)}) collective-permute-start(f32[4,128,128]{2,1,0:T(8,128)S(1)} %mask.1.own.state.refs_1_.refs_2_), channel_id=1, source_target_pairs={{0,4},{4,0},{8,12},{12,8},{16,20},{20,16},{24,28},{28,24},{32,36},... | collective-permute-start | bytes 786440 | tf_op jit(solution)/shard_map/ppermute | solution.py:239
  5.6 1.9 collective-permute-start
  13.3 1.9 terms.5
  15.2 1.5 near.5
  16.9 1.9 collective-permute-start.4
  21.1 4.0 %collective-permute-done.2.r1 = f32[4,128,128]{2,1,0:T(8,128)S(1)} collective-permute-done((f32[4,128,128]{2,1,0:T(8,128)S(1)}, f32[4,128,128]{2,1,0:T(8,128)S(1)}, u32[]{:S(2)}, u32[]{:S(2)}) %collective-permute-start.2) | collective-permute-done | bytes 262176 | tf_op jit(solution)/shard_map/ppermute | solution.py:233
  25.1 5.3 %collective-permute-done.4.r3 = f32[4,128,128]{2,1,0:T(8,128)S(1)} collective-permute-done((f32[4,128,128]{2,1,0:T(8,128)S(1)}, f32[4,128,128]{2,1,0:T(8,128)S(1)}, u32[]{:S(2)}, u32[]{:S(2)}) %collective-permute-start.4) | collective-permute-done | bytes 262176 | tf_op jit(solution)/shard_map/ppermute | solution.py:233
  30.6 27.4 %all_to_all.25 = f32[256,1,128]{2,1,0:T(1,128)S(1)} all-to-all(f32[256,1,128]{2,1,0:T(1,128)S(1)} %bitcast.33), channel_id=1, replica_groups=mesh['sec'=64,'pair'=4] {'sec','pair'}, dimensions={0} | all-to-all | bytes 262144 | tf_op jit(solution)/shard_map/all_to_all | solution.py:244
  59.1 2.1 collective-permute-start.5
  61.2 5.5 %collective-permute-done.5.by_chip = f32[4,128,128]{2,1,0:T(8,128)S(1)} collective-permute-done((f32[4,128,128]{2,1,0:T(8,128)S(1)}, f32[4,128,128]{2,1,0:T(8,128)S(1)}, u32[]{:S(2)}, u32[]{:S(2)}) %collective-permute-start.5) | collective-permute-done | bytes 262176 | tf_op jit(solution)/shard_map/ppermute | solution.py:238
  66.8 1.9 terms.6
  71.5 2.0 collective-permute-start.8
  75.5 4.1 %collective-permute-done.9.r3 = f32[4,128,128]{2,1,0:T(8,128)S(1)} collective-permute-done((f32[4,128,128]{2,1,0:T(8,128)S(1)}, f32[4,128,128]{2,1,0:T(8,128)S(1)}, u32[]{:S(2)}, u32[]{:S(2)}) %collective-permute-start.9) | collective-permute-done | bytes 262176 | tf_op jit(solution)/shard_map/ppermute | solution.py:233
  79.9 23.7 %all_to_all.26 = f32[256,1,128]{2,1,0:T(1,128)S(1)} all-to-all(f32[256,1,128]{2,1,0:T(1,128)S(1)} %bitcast.34), channel_id=1, replica_groups=mesh['sec'=64,'pair'=4] {'sec','pair'}, dimensions={0} | all-to-all | bytes 262144 | tf_op jit(solution)/shard_map/all_to_all | solution.py:244
  104.7 2.1 collective-permute-start.10
  106.8 5.5 %collective-permute-done.10.by_chip = f32[4,128,128]{2,1,0:T(8,128)S(1)} collective-permute-done((f32[4,128,128]{2,1,0:T(8,128)S(1)}, f32[4,128,128]{2,1,0:T(8,128)S(1)}, u32[]{:S(2)}, u32[]{:S(2)}) %collective-permute-start.10) | collective-permute-done | bytes 262176 | tf_op jit(solution)/shard_map/ppermute | solution.py:238
  112.4 1.9 terms.7
  117.1 2.0 collective-permute-start.13
  121.1 4.1 %collective-permute-done.14.r3 = f32[4,128,128]{2,1,0:T(8,128)S(1)} collective-permute-done((f32[4,128,128]{2,1,0:T(8,128)S(1)}, f32[4,128,128]{2,1,0:T(8,128)S(1)}, u32[]{:S(2)}, u32[]{:S(2)}) %collective-permute-start.14) | collective-permute-done | bytes 262176 | tf_op jit(solution)/shard_map/ppermute | solution.py:233
  125.5 23.7 %all_to_all.27 = f32[256,1,128]{2,1,0:T(1,128)S(1)} all-to-all(f32[256,1,128]{2,1,0:T(1,128)S(1)} %bitcast.35), channel_id=1, replica_groups=mesh['sec'=64,'pair'=4] {'sec','pair'}, dimensions={0} | all-to-all | bytes 262144 | tf_op jit(solution)/shard_map/all_to_all | solution.py:244
  150.4 2.1 collective-permute-start.15
  152.5 5.5 %collective-permute-done.15.by_chip = f32[4,128,128]{2,1,0:T(8,128)S(1)} collective-permute-done((f32[4,128,128]{2,1,0:T(8,128)S(1)}, f32[4,128,128]{2,1,0:T(8,128)S(1)}, u32[]{:S(2)}, u32[]{:S(2)}) %collective-permute-start.15) | collective-permute-done | bytes 262176 | tf_op jit(solution)/shard_map/ppermute | solution.py:238
  158.0 1.9 terms.8
  163.0 2.0 collective-permute-start.18
  167.0 4.1 %collective-permute-done.19.r3 = f32[4,128,128]{2,1,0:T(8,128)S(1)} collective-permute-done((f32[4,128,128]{2,1,0:T(8,128)S(1)}, f32[4,128,128]{2,1,0:T(8,128)S(1)}, u32[]{:S(2)}, u32[]{:S(2)}) %collective-permute-start.19) | collective-permute-done | bytes 262176 | tf_op jit(solution)/shard_map/ppermute | solution.py:233
  171.4 23.7 %all_to_all.28 = f32[256,1,128]{2,1,0:T(1,128)S(1)} all-to-all(f32[256,1,128]{2,1,0:T(1,128)S(1)} %bitcast.36), channel_id=1, replica_groups=mesh['sec'=64,'pair'=4] {'sec','pair'}, dimensions={0} | all-to-all | bytes 262144 | tf_op jit(solution)/shard_map/all_to_all | solution.py:244
  196.2 2.1 collective-permute-start.20
  198.4 5.5 %collective-permute-done.20.by_chip = f32[4,128,128]{2,1,0:T(8,128)S(1)} collective-permute-done((f32[4,128,128]{2,1,0:T(8,128)S(1)}, f32[4,128,128]{2,1,0:T(8,128)S(1)}, u32[]{:S(2)}, u32[]{:S(2)}) %collective-permute-start.20) | collective-permute-done | bytes 262176 | tf_op jit(solution)/shard_map/ppermute | solution.py:238
  203.9 1.9 terms.9
  208.6 2.0 collective-permute-start.23
  212.6 4.1 %collective-permute-done.24.r3 = f32[4,128,128]{2,1,0:T(8,128)S(1)} collective-permute-done((f32[4,128,128]{2,1,0:T(8,128)S(1)}, f32[4,128,128]{2,1,0:T(8,128)S(1)}, u32[]{:S(2)}, u32[]{:S(2)}) %collective-permute-start.24) | collective-permute-done | bytes 262176 | tf_op jit(solution)/shard_map/ppermute | solution.py:233
  217.6 23.7 %all_to_all.29 = f32[256,1,128]{2,1,0:T(1,128)S(1)} all-to-all(f32[256,1,128]{2,1,0:T(1,128)S(1)} %bitcast.32), channel_id=1, replica_groups=mesh['sec'=64,'pair'=4] {'sec','pair'}, dimensions={0} | all-to-all | bytes 262144 | tf_op jit(solution)/shard_map/all_to_all | solution.py:244
  (62 shorter events, 35.5 us)
Async XLA Ops:
  1.3 1.0 copy-start.2
  2.3 10.5 %collective-permute-start.1 = (f32[4,128,128]{2,1,0:T(8,128)S(1)}, f32[4,128,128]{2,1,0:T(8,128)S(1)}, u32[]{:S(2)}, u32[]{:S(2)}) collective-permute-start(f32[4,128,128]{2,1,0:T(8,128)S(1)} %mask.1.own.state.refs_1_.refs_2_), channel_id=1, source_target_pairs={{0,4},{4,0},{8,12},{12,8},{16,20},{20,16},{24,28},{28,24},{32,36},... | collective-permute-start | bytes 786440 | tf_op jit(solution)/shard_map/ppermute | solution.py:239
  5.6 7.7 %collective-permute-start = (f32[4,128,128]{2,1,0:T(8,128)S(1)}, f32[4,128,128]{2,1,0:T(8,128)S(1)}, u32[]{:S(2)}, u32[]{:S(2)}) collective-permute-start(f32[4,128,128]{2,1,0:T(8,128)S(1)} %mask.1.own.state.refs_1_.refs_2_), channel_id=1, source_target_pairs={{4,8},{8,4},{12,16},{16,12},{20,24},{24,20},{28,32},{32,28},{36,40... | collective-permute-start | bytes 786440 | tf_op jit(solution)/shard_map/ppermute | solution.py:238
  8.4 1.4 copy-start
  9.8 1.0 copy-start.1
  10.8 0.7 copy-start.3
  16.7 8.4 %collective-permute-start.2 = (f32[4,128,128]{2,1,0:T(8,128)S(1)}, f32[4,128,128]{2,1,0:T(8,128)S(1)}, u32[]{:S(2)}, u32[]{:S(2)}) collective-permute-start(f32[4,128,128]{2,1,0:T(8,128)S(1)} %get-tuple-element.53), channel_id=1, source_target_pairs={{0,1},{1,0},{2,3},{3,2},{4,5},{5,4},{6,7},{7,6},{8,9},{9,8},{10,11... | collective-permute-start | bytes 786440 | tf_op jit(solution)/shard_map/ppermute | solution.py:233
  16.9 13.5 %collective-permute-start.4 = (f32[4,128,128]{2,1,0:T(8,128)S(1)}, f32[4,128,128]{2,1,0:T(8,128)S(1)}, u32[]{:S(2)}, u32[]{:S(2)}) collective-permute-start(f32[4,128,128]{2,1,0:T(8,128)S(1)} %get-tuple-element.55), channel_id=1, source_target_pairs={{0,3},{1,2},{2,1},{3,0},{4,7},{5,6},{6,5},{7,4},{8,11},{9,10},{10,... | collective-permute-start | bytes 786440 | tf_op jit(solution)/shard_map/ppermute | solution.py:233
  18.8 11.6 %collective-permute-start.3 = (f32[4,128,128]{2,1,0:T(8,128)S(1)}, f32[4,128,128]{2,1,0:T(8,128)S(1)}, u32[]{:S(2)}, u32[]{:S(2)}) collective-permute-start(f32[4,128,128]{2,1,0:T(8,128)S(1)} %get-tuple-element.54), channel_id=1, source_target_pairs={{0,2},{1,3},{2,0},{3,1},{4,6},{5,7},{6,4},{7,5},{8,10},{9,11},{10,... | collective-permute-start | bytes 786440 | tf_op jit(solution)/shard_map/ppermute | solution.py:233
  21.1 45.7 %copy-start.4 = (s32[6]{0:T(128)S(1)}, s32[6]{0:T(128)}, u32[]{:S(2)}) copy-start(s32[6]{0:T(128)} %shift.11) | copy-start | bytes 76
  58.3 2.9 %collective-permute-start.6 = (f32[4,128,128]{2,1,0:T(8,128)S(1)}, f32[4,128,128]{2,1,0:T(8,128)S(1)}, u32[]{:S(2)}, u32[]{:S(2)}) collective-permute-start(f32[4,128,128]{2,1,0:T(8,128)S(1)} %get-tuple-element.59.own.corr.refs_5_), channel_id=1, source_target_pairs={{0,4},{4,0},{8,12},{12,8},{16,20},{20,16},{24,28},{28,24},{32,36},... | collective-permute-start | bytes 786440 | tf_op jit(solution)/shard_map/ppermute | solution.py:239
  59.1 7.7 %collective-permute-start.5 = (f32[4,128,128]{2,1,0:T(8,128)S(1)}, f32[4,128,128]{2,1,0:T(8,128)S(1)}, u32[]{:S(2)}, u32[]{:S(2)}) collective-permute-start(f32[4,128,128]{2,1,0:T(8,128)S(1)} %get-tuple-element.59.own.corr.refs_5_), channel_id=1, source_target_pairs={{4,8},{8,4},{12,16},{16,12},{20,24},{24,20},{28,32},{32,28},{36,40... | collective-permute-start | bytes 786440 | tf_op jit(solution)/shard_map/ppermute | solution.py:238
  70.2 5.3 %collective-permute-start.7 = (f32[4,128,128]{2,1,0:T(8,128)S(1)}, f32[4,128,128]{2,1,0:T(8,128)S(1)}, u32[]{:S(2)}, u32[]{:S(2)}) collective-permute-start(f32[4,128,128]{2,1,0:T(8,128)S(1)} %get-tuple-element.61), channel_id=1, source_target_pairs={{0,1},{1,0},{2,3},{3,2},{4,5},{5,4},{6,7},{7,6},{8,9},{9,8},{10,11... | collective-permute-start | bytes 786440 | tf_op jit(solution)/shard_map/ppermute | solution.py:233
  70.3 9.3 %collective-permute-start.9 = (f32[4,128,128]{2,1,0:T(8,128)S(1)}, f32[4,128,128]{2,1,0:T(8,128)S(1)}, u32[]{:S(2)}, u32[]{:S(2)}) collective-permute-start(f32[4,128,128]{2,1,0:T(8,128)S(1)} %get-tuple-element.63), channel_id=1, source_target_pairs={{0,3},{1,2},{2,1},{3,0},{4,7},{5,6},{6,5},{7,4},{8,11},{9,10},{10,... | collective-permute-start | bytes 786440 | tf_op jit(solution)/shard_map/ppermute | solution.py:233
  71.5 8.1 %collective-permute-start.8 = (f32[4,128,128]{2,1,0:T(8,128)S(1)}, f32[4,128,128]{2,1,0:T(8,128)S(1)}, u32[]{:S(2)}, u32[]{:S(2)}) collective-permute-start(f32[4,128,128]{2,1,0:T(8,128)S(1)} %get-tuple-element.62), channel_id=1, source_target_pairs={{0,2},{1,3},{2,0},{3,1},{4,6},{5,7},{6,4},{7,5},{8,10},{9,11},{10,... | collective-permute-start | bytes 786440 | tf_op jit(solution)/shard_map/ppermute | solution.py:233
  103.9 2.9 %collective-permute-start.11 = (f32[4,128,128]{2,1,0:T(8,128)S(1)}, f32[4,128,128]{2,1,0:T(8,128)S(1)}, u32[]{:S(2)}, u32[]{:S(2)}) collective-permute-start(f32[4,128,128]{2,1,0:T(8,128)S(1)} %get-tuple-element.67.own.corr.refs_5_), channel_id=1, source_target_pairs={{0,4},{4,0},{8,12},{12,8},{16,20},{20,16},{24,28},{28,24},{32,36},... | collective-permute-start | bytes 786440 | tf_op jit(solution)/shard_map/ppermute | solution.py:239
  104.7 7.7 %collective-permute-start.10 = (f32[4,128,128]{2,1,0:T(8,128)S(1)}, f32[4,128,128]{2,1,0:T(8,128)S(1)}, u32[]{:S(2)}, u32[]{:S(2)}) collective-permute-start(f32[4,128,128]{2,1,0:T(8,128)S(1)} %get-tuple-element.67.own.corr.refs_5_), channel_id=1, source_target_pairs={{4,8},{8,4},{12,16},{16,12},{20,24},{24,20},{28,32},{32,28},{36,40... | collective-permute-start | bytes 786440 | tf_op jit(solution)/shard_map/ppermute | solution.py:238
  115.8 5.3 %collective-permute-start.12 = (f32[4,128,128]{2,1,0:T(8,128)S(1)}, f32[4,128,128]{2,1,0:T(8,128)S(1)}, u32[]{:S(2)}, u32[]{:S(2)}) collective-permute-start(f32[4,128,128]{2,1,0:T(8,128)S(1)} %get-tuple-element.69), channel_id=1, source_target_pairs={{0,1},{1,0},{2,3},{3,2},{4,5},{5,4},{6,7},{7,6},{8,9},{9,8},{10,11... | collective-permute-start | bytes 786440 | tf_op jit(solution)/shard_map/ppermute | solution.py:233
  115.9 9.3 %collective-permute-start.14 = (f32[4,128,128]{2,1,0:T(8,128)S(1)}, f32[4,128,128]{2,1,0:T(8,128)S(1)}, u32[]{:S(2)}, u32[]{:S(2)}) collective-permute-start(f32[4,128,128]{2,1,0:T(8,128)S(1)} %get-tuple-element.71), channel_id=1, source_target_pairs={{0,3},{1,2},{2,1},{3,0},{4,7},{5,6},{6,5},{7,4},{8,11},{9,10},{10,... | collective-permute-start | bytes 786440 | tf_op jit(solution)/shard_map/ppermute | solution.py:233
  117.1 8.1 %collective-permute-start.13 = (f32[4,128,128]{2,1,0:T(8,128)S(1)}, f32[4,128,128]{2,1,0:T(8,128)S(1)}, u32[]{:S(2)}, u32[]{:S(2)}) collective-permute-start(f32[4,128,128]{2,1,0:T(8,128)S(1)} %get-tuple-element.70), channel_id=1, source_target_pairs={{0,2},{1,3},{2,0},{3,1},{4,6},{5,7},{6,4},{7,5},{8,10},{9,11},{10,... | collective-permute-start | bytes 786440 | tf_op jit(solution)/shard_map/ppermute | solution.py:233
  149.6 2.9 %collective-permute-start.16 = (f32[4,128,128]{2,1,0:T(8,128)S(1)}, f32[4,128,128]{2,1,0:T(8,128)S(1)}, u32[]{:S(2)}, u32[]{:S(2)}) collective-permute-start(f32[4,128,128]{2,1,0:T(8,128)S(1)} %get-tuple-element.77.own.corr.refs_5_), channel_id=1, source_target_pairs={{0,4},{4,0},{8,12},{12,8},{16,20},{20,16},{24,28},{28,24},{32,36},... | collective-permute-start | bytes 786440 | tf_op jit(solution)/shard_map/ppermute | solution.py:239
  150.4 7.7 %collective-permute-start.15 = (f32[4,128,128]{2,1,0:T(8,128)S(1)}, f32[4,128,128]{2,1,0:T(8,128)S(1)}, u32[]{:S(2)}, u32[]{:S(2)}) collective-permute-start(f32[4,128,128]{2,1,0:T(8,128)S(1)} %get-tuple-element.77.own.corr.refs_5_), channel_id=1, source_target_pairs={{4,8},{8,4},{12,16},{16,12},{20,24},{24,20},{28,32},{32,28},{36,40... | collective-permute-start | bytes 786440 | tf_op jit(solution)/shard_map/ppermute | solution.py:238
  161.4 5.5 %collective-permute-start.17 = (f32[4,128,128]{2,1,0:T(8,128)S(1)}, f32[4,128,128]{2,1,0:T(8,128)S(1)}, u32[]{:S(2)}, u32[]{:S(2)}) collective-permute-start(f32[4,128,128]{2,1,0:T(8,128)S(1)} %get-tuple-element.79), channel_id=1, source_target_pairs={{0,1},{1,0},{2,3},{3,2},{4,5},{5,4},{6,7},{7,6},{8,9},{9,8},{10,11... | collective-permute-start | bytes 786440 | tf_op jit(solution)/shard_map/ppermute | solution.py:233
  161.8 9.3 %collective-permute-start.19 = (f32[4,128,128]{2,1,0:T(8,128)S(1)}, f32[4,128,128]{2,1,0:T(8,128)S(1)}, u32[]{:S(2)}, u32[]{:S(2)}) collective-permute-start(f32[4,128,128]{2,1,0:T(8,128)S(1)} %get-tuple-element.81), channel_id=1, source_target_pairs={{0,3},{1,2},{2,1},{3,0},{4,7},{5,6},{6,5},{7,4},{8,11},{9,10},{10,... | collective-permute-start | bytes 786440 | tf_op jit(solution)/shard_map/ppermute | solution.py:233
  163.0 8.1 %collective-permute-start.18 = (f32[4,128,128]{2,1,0:T(8,128)S(1)}, f32[4,128,128]{2,1,0:T(8,128)S(1)}, u32[]{:S(2)}, u32[]{:S(2)}) collective-permute-start(f32[4,128,128]{2,1,0:T(8,128)S(1)} %get-tuple-element.80), channel_id=1, source_target_pairs={{0,2},{1,3},{2,0},{3,1},{4,6},{5,7},{6,4},{7,5},{8,10},{9,11},{10,... | collective-permute-start | bytes 786440 | tf_op jit(solution)/shard_map/ppermute | solution.py:233
  195.4 2.9 %collective-permute-start.21 = (f32[4,128,128]{2,1,0:T(8,128)S(1)}, f32[4,128,128]{2,1,0:T(8,128)S(1)}, u32[]{:S(2)}, u32[]{:S(2)}) collective-permute-start(f32[4,128,128]{2,1,0:T(8,128)S(1)} %get-tuple-element.87.own.corr.refs_3_), channel_id=1, source_target_pairs={{0,4},{4,0},{8,12},{12,8},{16,20},{20,16},{24,28},{28,24},{32,36},... | collective-permute-start | bytes 786440 | tf_op jit(solution)/shard_map/ppermute | solution.py:239
  196.2 7.7 %collective-permute-start.20 = (f32[4,128,128]{2,1,0:T(8,128)S(1)}, f32[4,128,128]{2,1,0:T(8,128)S(1)}, u32[]{:S(2)}, u32[]{:S(2)}) collective-permute-start(f32[4,128,128]{2,1,0:T(8,128)S(1)} %get-tuple-element.87.own.corr.refs_3_), channel_id=1, source_target_pairs={{4,8},{8,4},{12,16},{16,12},{20,24},{24,20},{28,32},{32,28},{36,40... | collective-permute-start | bytes 786440 | tf_op jit(solution)/shard_map/ppermute | solution.py:238
  207.3 5.3 %collective-permute-start.22 = (f32[4,128,128]{2,1,0:T(8,128)S(1)}, f32[4,128,128]{2,1,0:T(8,128)S(1)}, u32[]{:S(2)}, u32[]{:S(2)}) collective-permute-start(f32[4,128,128]{2,1,0:T(8,128)S(1)} %get-tuple-element.89), channel_id=1, source_target_pairs={{0,1},{1,0},{2,3},{3,2},{4,5},{5,4},{6,7},{7,6},{8,9},{9,8},{10,11... | collective-permute-start | bytes 786440 | tf_op jit(solution)/shard_map/ppermute | solution.py:233
  207.4 9.3 %collective-permute-start.24 = (f32[4,128,128]{2,1,0:T(8,128)S(1)}, f32[4,128,128]{2,1,0:T(8,128)S(1)}, u32[]{:S(2)}, u32[]{:S(2)}) collective-permute-start(f32[4,128,128]{2,1,0:T(8,128)S(1)} %get-tuple-element.91), channel_id=1, source_target_pairs={{0,3},{1,2},{2,1},{3,0},{4,7},{5,6},{6,5},{7,4},{8,11},{9,10},{10,... | collective-permute-start | bytes 786440 | tf_op jit(solution)/shard_map/ppermute | solution.py:233
  208.6 8.1 %collective-permute-start.23 = (f32[4,128,128]{2,1,0:T(8,128)S(1)}, f32[4,128,128]{2,1,0:T(8,128)S(1)}, u32[]{:S(2)}, u32[]{:S(2)}) collective-permute-start(f32[4,128,128]{2,1,0:T(8,128)S(1)} %get-tuple-element.90), channel_id=1, source_target_pairs={{0,2},{1,3},{2,0},{3,1},{4,6},{5,7},{6,4},{7,5},{8,10},{9,11},{10,... | collective-permute-start | bytes 786440 | tf_op jit(solution)/shard_map/ppermute | solution.py:233

commit v3 on v2

v3 whole, which is shorter than its diff:
```python
import jax
import jax.numpy as jnp
from jax import lax
from jax.experimental import pallas as pl
from jax.experimental.pallas import tpu as pltpu
from jax.sharding import PartitionSpec as P

ITERS = 4
ROWS = 1
TERMS = 6
LOCAL = 4
GROUPS = 4
B = 128
PACK = LOCAL * B + 8

f32 = jnp.float32
bf16 = jnp.bfloat16
VM = pl.BlockSpec(memory_space=pltpu.VMEM)
SM = pl.BlockSpec(memory_space=pltpu.SMEM)
ANY = pl.BlockSpec(memory_space=pl.ANY)
PARAMS = pltpu.CompilerParams(vmem_limit_bytes=24 * 1024 * 1024)


def halves(x):
    high = x.astype(bf16)
    return high, (x - high.astype(f32)).astype(bf16)


def eye_mask():
    return lax.broadcasted_iota(jnp.int32, (B, B), 0) == lax.broadcasted_iota(jnp.int32, (B, B), 1)


def row_mask(rows):
    return (lax.broadcasted_iota(jnp.int32, (B, B), 0) < rows[0]).astype(f32)


def mask_kernel(rows, psi, state):
    keep = row_mask(rows)
    for p in range(LOCAL):
        state[p] = psi[p] * keep


def outer(left_lines, right_lines):
    return lax.dot_general(
        left_lines, right_lines, (((0,), (0,)), ((), ())),
        precision=lax.Precision.HIGHEST, preferred_element_type=f32)


def split_kernel(group, shift, rows, weights, left, right, left2, right2, diag, left_diag, right_diag,
                 left_buf, right_buf, sems):
    copies = [pltpu.make_async_copy(left, left_buf, sems.at[TERMS])]
    copies += [pltpu.make_async_copy(right.at[k], right_buf.at[k], sems.at[k]) for k in range(TERMS)]
    for copy in copies:
        copy.start()
    keep = row_mask(rows)
    eye = eye_mask()
    pad = jnp.zeros((8 - TERMS, B), f32)
    lines = []
    copies[0].wait()
    for k in range(TERMS):
        block = left_buf[k] * keep
        left2[k] = jnp.concatenate(halves(block), axis=1)
        chosen = jnp.where(shift[k] == 0, 1.0, 0.0).astype(f32)
        lines.append(jnp.sum(jnp.where(eye, block, 0.0), axis=0, keepdims=True) * chosen)
    left_diag[...] = jnp.concatenate(lines + [pad], axis=0)
    lines = [[] for _ in range(LOCAL)]
    for k in range(TERMS):
        copies[1 + k].wait()
        for q in range(LOCAL):
            block = right_buf[k, q]
            right2[k, q] = jnp.concatenate(halves(jnp.transpose(block)), axis=1)
            p = group[0] * LOCAL + q
            scale = weights[k * 256 + p * 16 + p]
            lines[q].append(jnp.sum(jnp.where(eye, block, 0.0), axis=0, keepdims=True) * scale)
    for q in range(LOCAL):
        right_diag[q] = jnp.concatenate(lines[q] + [pad], axis=0)
        diag[q] = outer(left_diag[...], right_diag[q])


def mix(group, weights, z, out, target, at_out=0):
    for half in range(2):
        first = target * LOCAL + 2 * half
        acc = [None, None]
        for k in range(TERMS):
            for q in range(LOCAL):
                block = z[k * LOCAL + q]
                for j in range(2):
                    at = k * 256 + (first + j) * 16 + group[0] * LOCAL + q
                    part = weights[at] * block
                    acc[j] = part if acc[j] is None else acc[j] + part
        for j in range(2):
            out[at_out + 2 * half + j] = acc[j]


def terms_kernel(group, sector, shift, weights, own, by_chip, by_core, left2, right2, z, out, vec2):
    odd = lax.rem(sector[0], 2)
    for p in range(LOCAL):
        vec2[1, p] = jnp.concatenate(halves(own[p]), axis=1)
        vec2[2 - 2 * odd, p] = jnp.concatenate(halves(by_core[p]), axis=1)
        vec2[2 * odd, p] = jnp.concatenate(halves(by_chip[p]), axis=1)
    for k in range(TERMS):
        source = shift[k] + 1
        lhs = left2[k]
        for q in range(LOCAL):
            r = right2[k, q]
            x = jnp.dot(vec2[source, q], jnp.concatenate([r, r], axis=0), preferred_element_type=f32)
            xh, xl = halves(x[:, :B] + x[:, B:])
            both = jnp.concatenate([xh, xl], axis=1)
            y = jnp.dot(lhs, jnp.concatenate([both, both], axis=0), preferred_element_type=f32)
            z[k * LOCAL + q] = y[:, :B] + y[:, B:]
    mix(group, weights, z, out, group[0] ^ (1 + 2 * odd))
    mix(group, weights, z, out, group[0] ^ 2, LOCAL)


def rest_kernel(group, sector, weights, z, own, onward):
    odd = lax.rem(sector[0], 2)
    mix(group, weights, z, own, group[0])
    mix(group, weights, z, onward, group[0] ^ (3 - 2 * odd))


def onward_kernel(onward, first, out):
    for p in range(LOCAL):
        out[p] = onward[p] + first[LOCAL + p]


def lane(row, j):
    at = lax.broadcasted_iota(jnp.int32, row.shape, 1) == j
    return jnp.sum(jnp.where(at, row, 0.0), axis=1, keepdims=True)


def put_lanes(values):
    at = lax.broadcasted_iota(jnp.int32, (1, B), 1)
    row = jnp.zeros((1, B), f32)
    for j, v in enumerate(values):
        row = jnp.where(at == j, v, row)
    return row


def lowest_root(lead, middle, const):
    root = jnp.sqrt(middle * middle - 4.0 * lead * const)
    return jnp.where(middle > 0, (-middle - root) / (2.0 * lead), 2.0 * const / (root - middle))


def ritz(sums, rayleigh, length):
    s_ic, c_i, curvature, correlation, spread = sums
    cross = 0.5 * (s_ic + c_i)
    lead = length * spread - correlation * correlation
    middle = -(length * curvature + spread * rayleigh - 2.0 * correlation * cross)
    const = rayleigh * curvature - cross * cross
    lowest = lowest_root(lead, middle, const)
    keep = curvature - lowest * spread
    add = lowest * correlation - cross
    norm = keep * keep * length + 2.0 * keep * add * correlation + add * add * spread
    factor = 1.0 / jnp.sqrt(norm)
    keep, add = keep * factor, add * factor
    rayleigh = keep * keep * rayleigh + 2.0 * keep * add * cross + add * add * curvature
    length = keep * keep * length + 2.0 * keep * add * correlation + add * add * spread
    return lowest, keep, add, rayleigh, length


def totals(stats, count, n):
    row = jnp.sum(stats[...], axis=0, keepdims=True) * (1.0 / (ROWS * count))
    return [lane(row, j) for j in range(n)]


def correct(state, image, diag, theta):
    return (image - theta * state) / jnp.maximum(jnp.abs(diag - theta), 1.0)


def start_kernel(count, stats, s0, s1, s2, pack0, pack1, pack2, diag0, right_diag,
                 i0, i1, i2, diag1, diag2, c0, c1, c2, carry):
    rayleigh, length = totals(stats, count, 2)
    theta = rayleigh / length
    for pack, diag in ((pack1, diag1), (pack2, diag2)):
        for p in range(LOCAL):
            diag[p] = outer(pack[LOCAL * B:PACK, :], right_diag[p])
    for s, pack, i, diag, c in ((s0, pack0, i0, diag0, c0), (s1, pack1, i1, diag1, c1), (s2, pack2, i2, diag2, c2)):
        for p in range(LOCAL):
            block = pack[p * B:(p + 1) * B, :]
            i[p] = block
            c[p] = correct(s[p], block, diag[p], theta)
    carry[...] = jnp.broadcast_to(put_lanes([rayleigh, length]), (8, B))


def next_kernel(count, step, stats, carry_in, *refs):
    sums = totals(stats, count, 5)
    old = carry_in[0:1, :]
    lowest, keep, add, rayleigh, length = ritz(sums, lane(old, 0), lane(old, 1))
    theta = rayleigh / length
    for n in range(3):
        state, image, corr, diag, more, state_out, image_out, corr_out = refs[n:24:3]
        for p in range(LOCAL):
            s = keep * state[p] + add * corr[p]
            i = keep * image[p] + add * more[p]
            state_out[p] = s
            image_out[p] = i
            corr_out[p] = correct(s, i, diag[p], theta)
    energies = [lane(old, 2 + j) for j in range(step)] + [lowest]
    refs[24][...] = jnp.broadcast_to(put_lanes([rayleigh, length] + energies), (8, B))


def last_kernel(count, stats, carry_in, state, corr, state_out, energies):
    sums = totals(stats, count, 5)
    old = carry_in[0:1, :]
    lowest, keep, add, _, _ = ritz(sums, lane(old, 0), lane(old, 1))
    for p in range(LOCAL):
        state_out[p] = keep * state[p] + add * corr[p]
    for j, v in enumerate([lane(old, 2 + j) for j in range(ITERS - 1)] + [lowest]):
        energies[j] = v[0, 0]


def sum_all(block):
    return jnp.sum(jnp.sum(block, axis=0, keepdims=True), axis=1, keepdims=True)


def first_stats_kernel(own, first, second, state, stats):
    a, b = jnp.zeros((B, B), f32), jnp.zeros((B, B), f32)
    for p in range(LOCAL):
        i = (own[p] + first[p]) + second[p]
        s = state[p]
        a = a + s * i
        b = b + s * s
    stats[...] = jnp.broadcast_to(put_lanes([sum_all(a), sum_all(b)]), stats.shape)


def first_sum_kernel(own, first, second, left_diag, stats, pack):
    for p in range(LOCAL):
        pack[p * B:(p + 1) * B, :] = (own[p] + first[p]) + second[p]
    pack[LOCAL * B:PACK, :] = left_diag[...]


def stats_kernel(own, first, second, state, corr, image, stats):
    acc = [jnp.zeros((B, B), f32) for _ in range(5)]
    for p in range(LOCAL):
        ic = (own[p] + first[p]) + second[p]
        s, c, i = state[p], corr[p], image[p]
        for j, v in enumerate((s * ic, c * i, c * ic, s * c, c * c)):
            acc[j] = acc[j] + v
    stats[...] = jnp.broadcast_to(put_lanes([sum_all(a) for a in acc]), stats.shape)


def sum_kernel(own, first, second, stats, image_corr):
    for p in range(LOCAL):
        image_corr[p] = (own[p] + first[p]) + second[p]


def arr(*shape, dtype=f32):
    return jax.ShapeDtypeStruct(shape, dtype)


BLOCK = arr(LOCAL, B, B)
TERM_BLOCKS = arr(TERMS * LOCAL, B, B)


def call(kernel, name, in_specs, outs, scratch=(), out_specs=None, flops=0):
    moved = sum(o.size * o.dtype.itemsize for o in outs)
    return pl.pallas_call(
        kernel,
        out_shape=outs,
        in_specs=in_specs,
        out_specs=out_specs or [VM] * len(outs),
        scratch_shapes=list(scratch),
        compiler_params=PARAMS,
        cost_estimate=pl.CostEstimate(flops=flops, bytes_accessed=2 * moved, transcendentals=0),
        name=name,
    )


def swap(x, even, odd):
    n = lax.axis_size("sec")
    perm = [(s * GROUPS + g, s * GROUPS + (g ^ (odd if s % 2 else even))) for s in range(n) for g in range(GROUPS)]
    return lax.ppermute(x, ("sec", "pair"), perm)


def neighbours(x):
    n = lax.axis_size("sec")
    by_chip = lax.ppermute(x, "sec", [(i, i + 1 if i % 2 else i - 1) for i in range(1, n - 1)])
    by_core = lax.ppermute(x, "sec", [(i, i ^ 1) for i in range(n)])
    return by_chip, by_core


def exchange(stats, devices):
    got = lax.all_to_all(stats.reshape(devices, ROWS, B), ("sec", "pair"), 0, 0)
    return got.reshape(ROWS * devices, B)


def on_device(psi_start, left_env, right_env, mpo_coef, mpo_pattern, sector_shift, block_rows):
    devices = lax.axis_size("sec") * lax.axis_size("pair")
    count = float(psi_start.size * devices)
    psi = psi_start.reshape(LOCAL, B, B)
    left = left_env.reshape(TERMS, B, B)
    group = lax.axis_index("pair").astype(jnp.int32).reshape(1)
    sector = lax.axis_index("sec").astype(jnp.int32).reshape(1)
    weights = (mpo_coef * mpo_pattern.astype(f32)).reshape(-1)
    stats_shape = arr(ROWS * devices, B)
    carry_shape = arr(8, B)

    def shares(vectors, left2, right2):
        z, part = call(
            terms_kernel, "terms", [SM] * 4 + [VM] * 5, [TERM_BLOCKS, arr(2 * LOCAL, B, B)],
            [pltpu.VMEM((3, LOCAL, B, 2 * B), bf16)],
        )(group, sector, sector_shift, weights, *vectors, left2, right2)
        first = swap(part, 1, 3)
        own, onward = call(rest_kernel, "rest", [SM] * 3 + [VM], [BLOCK] * 2)(group, sector, weights, z)
        (onward,) = call(onward_kernel, "onward", [VM] * 2, [BLOCK])(onward, first)
        return own, first, swap(onward, 3, 1)

    (state,) = call(mask_kernel, "mask", [SM, VM], [BLOCK])(block_rows, psi)
    states = (state, *neighbours(state))
    left2, right2, diag, left_diag, right_diag = call(
        split_kernel, "split", [SM] * 4 + [ANY] * 2,
        [arr(TERMS, B, 2 * B, dtype=bf16), arr(TERMS, LOCAL, B, 2 * B, dtype=bf16), BLOCK, arr(8, B), arr(LOCAL, 8, B)],
        [pltpu.VMEM((TERMS, B, B), f32), pltpu.VMEM((TERMS, LOCAL, B, B), f32), pltpu.SemaphoreType.DMA((TERMS + 1,))],
    )(group, sector_shift, block_rows, weights, left, right_env)

    parts = shares(states, left2, right2)
    (stats,) = call(first_stats_kernel, "first_stats", [VM] * 4, [stats_shape])(*parts, state)
    (pack,) = call(first_sum_kernel, "first_sum", [VM] * 4 + [ANY], [arr(PACK, B)])(*parts, left_diag, stats)
    packs = (pack, *neighbours(pack))
    *out, carry = call(
        lambda *refs: start_kernel(count, *refs), "start", [VM] * 9, [BLOCK] * 8 + [carry_shape]
    )(exchange(stats, devices), *states, *packs, diag, right_diag)
    images, diags, corrs = out[:3], (diag, *out[3:5]), out[5:8]

    for step in range(ITERS):
        parts = shares(corrs, left2, right2)
        (stats,) = call(stats_kernel, "stats", [VM] * 6, [stats_shape])(*parts, states[0], corrs[0], images[0])
        got = exchange(stats, devices)
        if step < ITERS - 1:
            (image_corr,) = call(sum_kernel, "sum", [VM] * 3 + [ANY], [BLOCK])(*parts, stats)
            more = (image_corr, *neighbours(image_corr))
            *out, carry = call(
                lambda *refs, step=step: next_kernel(count, step, *refs), "next", [VM] * 17, [BLOCK] * 9 + [carry_shape]
            )(got, carry, *states, *images, *corrs, *diags, *more)
            states, images, corrs = out[:3], out[3:6], out[6:9]

    state, energies = call(
        lambda *refs: last_kernel(count, *refs), "last", [VM] * 4, [BLOCK, arr(ITERS)], out_specs=[VM, SM]
    )(got, carry, states[0], corrs[0])
    return state.reshape(psi_start.shape), energies


def solution(mesh):
    in_specs = (
        P("sec", "pair", None, None),
        P(None, "sec", None, None),
        P(None, "pair", None, None),
        P(),
        P(),
        P(),
        P("sec"),
    )
    out_specs = (P("sec", "pair", None, None), P())
    return jax.shard_map(
        on_device, mesh=mesh, in_specs=in_specs, out_specs=out_specs, check_vma=False
    )
```

time: 243 us -> 233 us (0.959)
  blocking collectives: 122 us -> 104 us
  waiting for transfers between devices: 52.2 us -> 60.3 us
    ppermute x15 -> x10, waiting for transfers between devices: 29.5 us -> 60.3 us  [swap(): return lax.ppermute(x, ('sec', 'pair'), perm)]
    ppermute x5, waiting for transfers between devices: 22.7 us -> 0.01 us  [neighbours(): lax.ppermute(x, 'sec', [(i, i + 1 if i % 2 else i - 1) for i in range(1,...]
    all_to_all x5, blocking collectives: 122 us -> 104 us  [exchange(): got = lax.all_to_all(stats.reshape(devices, ROWS, B), ('sec', 'pair'), 0, 0)]
    ppermute x15 -> x10, starting transfers between devices: 16.9 us -> 7.17 us  [swap(): return lax.ppermute(x, ('sec', 'pair'), perm)]
    ppermute x5, starting transfers between devices: 6.54 us -> 12.6 us  [neighbours(): by_core = lax.ppermute(x, 'sec', [(i, i ^ 1) for i in range(n)])]
    ppermute x5, starting transfers between devices: 10.4 us -> 13.1 us  [neighbours(): lax.ppermute(x, 'sec', [(i, i + 1 if i % 2 else i - 1) for i in range(1,...]
    pallas_call x22 -> x26, Pallas kernels: 25.6 us -> 24.7 us  [the longest x5 12.9 us: shares(): call(terms_kernel, 'terms', [SM] * 4 + [VM] * 5, [TERM_BLOCKS, arr(2 * LO...]
  transfers between devices with their start and end apart: 25 -> 20, of which waited for: 15 -> 10; matrix products, arithmetic and copies ran while one was open for 0% -> 0% of each run, Pallas kernels for 3% -> 4%
where the time goes in v3:
time: 233 us; the launch traced here: 232 us
  blocking collectives  104 us (45%)
  waiting for transfers between devices  60.3 us (26%)
  starting transfers between devices  32.9 us (14%)
  Pallas kernels  28.1 us (12%)
  local copies, waits for them, and re-layouts  4.13 us (2%)
    all_to_all x5, blocking collectives, exchange(): got = lax.all_to_all(stats.reshape(devices, ROWS, B), ('sec', 'pair'), 0, 0)  104 us
    ppermute x10, waiting for transfers between devices, swap(): return lax.ppermute(x, ('sec', 'pair'), perm)  60.3 us
    ppermute x5, starting transfers between devices, neighbours(): lax.ppermute(x, 'sec', [(i, i + 1 if i % 2 else i - 1) for i in range(1,...  13.1 us
    pallas_call x5, Pallas kernels, shares(): call(terms_kernel, 'terms', [SM] * 4 + [VM] * 5, [TERM_BLOCKS, arr(2 * LO...  12.9 us
    ppermute x5, starting transfers between devices, neighbours(): by_core = lax.ppermute(x, 'sec', [(i, i ^ 1) for i in range(n)])  12.6 us
    pallas_call x5, Pallas kernels, shares(): call(rest_kernel, 'rest', [SM] * 3 + [VM], [BLOCK] * 2)  7.34 us
    ppermute x10, starting transfers between devices, swap(): return lax.ppermute(x, ('sec', 'pair'), perm)  7.17 us
  transfers between devices with their start and end apart: 20, of which 10 were waited for; matrix products, arithmetic and copies ran while one was open for 0% of the time, Pallas kernels for 4%

profile of v3, /device:TPU:1, one launch (start us, length us, event | category | flops | bytes accessed | tf_op | source)
XLA Modules:
  0.0 232.5 jit_solution(181416597116124786)
XLA Ops:
  2.3 3.3 %collective-permute-start.1 = (f32[4,128,128]{2,1,0:T(8,128)S(1)}, f32[4,128,128]{2,1,0:T(8,128)S(1)}, u32[]{:S(2)}, u32[]{:S(2)}) collective-permute-start(f32[4,128,128]{2,1,0:T(8,128)S(1)} %mask.1.own.state.refs_1_.refs_2_), channel_id=1, source_target_pairs={{0,4},{4,0},{8,12},{12,8},{16,20},{20,16},{24,28},{28,24},{32,36},... | collective-permute-start | bytes 786440 | tf_op jit(solution)/shard_map/ppermute | solution.py:278
  5.6 1.9 collective-permute-start
  11.5 2.2 split.1
  13.8 2.6 %terms.5 = (f32[24,128,128]{2,1,0:T(8,128)S(1)}, f32[8,128,128]{2,1,0:T(8,128)S(1)}) custom-call(s32[1]{0:T(128)} %bitcast.group, s32[1]{0:T(128)} %bitcast.1.sector, s32[6]{0:T(128)S(1)} %copy-done.3, f32[1536]{0:T(1024)S(1)} %reshape.54.weights, f32[4,128,128]{2,1,0:T(8,128)S(1)} %mask.1.own.state.refs_1_.refs_2_, ...), custom_call_target="tpu_custom_call" | custom-call | bytes 4194304 | tf_op jit(solution)/shard_map/terms/pallas_call | solution.py:299
  16.3 2.2 collective-permute-start.2
  18.5 1.5 rest.5
  20.0 5.7 %collective-permute-done.2.first = f32[8,128,128]{2,1,0:T(8,128)S(1)} collective-permute-done((f32[8,128,128]{2,1,0:T(8,128)S(1)}, f32[8,128,128]{2,1,0:T(8,128)S(1)}, u32[]{:S(2)}, u32[]{:S(2)}) %collective-permute-start.2) | collective-permute-done | bytes 524320 | tf_op jit(solution)/shard_map/ppermute | solution.py:272
  25.8 5.5 %collective-permute-done.3.second = f32[4,128,128]{2,1,0:T(8,128)S(1)} collective-permute-done((f32[4,128,128]{2,1,0:T(8,128)S(1)}, f32[4,128,128]{2,1,0:T(8,128)S(1)}, u32[]{:S(2)}, u32[]{:S(2)}) %collective-permute-start.3) | collective-permute-done | bytes 262176 | tf_op jit(solution)/shard_map/ppermute | solution.py:272
  32.4 4.9 %collective-permute-start.4 = (f32[520,128]{1,0:T(8,128)S(1)}, f32[520,128]{1,0:T(8,128)S(1)}, u32[]{:S(2)}, u32[]{:S(2)}) collective-permute-start(f32[520,128]{1,0:T(8,128)S(1)} %first_sum.1.refs_4_), channel_id=1, source_target_pairs={{4,8},{8,4},{12,16},{16,12},{20,24},{24,20},{28,32},{32,28},{36,40... | collective-permute-start | bytes 798728 | tf_op jit(solution)/shard_map/ppermute | solution.py:277
  37.3 26.7 %all_to_all.25 = f32[256,1,128]{2,1,0:T(1,128)S(1)} all-to-all(f32[256,1,128]{2,1,0:T(1,128)S(1)} %bitcast.25), channel_id=1, replica_groups=mesh['sec'=64,'pair'=4] {'sec','pair'}, dimensions={0} | all-to-all | bytes 262144 | tf_op jit(solution)/shard_map/all_to_all | solution.py:283
  64.8 2.6 %terms.6 = (f32[24,128,128]{2,1,0:T(8,128)S(1)}, f32[8,128,128]{2,1,0:T(8,128)S(1)}) custom-call(s32[1]{0:T(128)} %bitcast.group, s32[1]{0:T(128)} %bitcast.1.sector, s32[6]{0:T(128)S(1)} %copy-done.3, f32[1536]{0:T(1024)S(1)} %reshape.54.weights, f32[4,128,128]{2,1,0:T(8,128)S(1)} %get-tuple-element.73.own.corr.refs_8_, ...), custom_call_target="tpu_custom_call" | custom-call | bytes 4194304 | tf_op jit(solution)/shard_map/terms/pallas_call | solution.py:299
  70.1 6.8 %collective-permute-done.6.first = f32[8,128,128]{2,1,0:T(8,128)S(1)} collective-permute-done((f32[8,128,128]{2,1,0:T(8,128)S(1)}, f32[8,128,128]{2,1,0:T(8,128)S(1)}, u32[]{:S(2)}, u32[]{:S(2)}) %collective-permute-start.6) | collective-permute-done | bytes 524320 | tf_op jit(solution)/shard_map/ppermute | solution.py:272
  77.0 5.5 %collective-permute-done.7.second = f32[4,128,128]{2,1,0:T(8,128)S(1)} collective-permute-done((f32[4,128,128]{2,1,0:T(8,128)S(1)}, f32[4,128,128]{2,1,0:T(8,128)S(1)}, u32[]{:S(2)}, u32[]{:S(2)}) %collective-permute-start.7) | collective-permute-done | bytes 262176 | tf_op jit(solution)/shard_map/ppermute | solution.py:272
  82.8 2.8 %collective-permute-start.9 = (f32[4,128,128]{2,1,0:T(8,128)S(1)}, f32[4,128,128]{2,1,0:T(8,128)S(1)}, u32[]{:S(2)}, u32[]{:S(2)}) collective-permute-start(f32[4,128,128]{2,1,0:T(8,128)S(1)} %sum.3.refs_14_), channel_id=1, source_target_pairs={{0,4},{4,0},{8,12},{12,8},{16,20},{20,16},{24,28},{28,24},{32,36},... | collective-permute-start | bytes 786440 | tf_op jit(solution)/shard_map/ppermute | solution.py:278
  85.6 2.1 collective-permute-start.8
  87.7 19.1 %all_to_all.26 = f32[256,1,128]{2,1,0:T(1,128)S(1)} all-to-all(f32[256,1,128]{2,1,0:T(1,128)S(1)} %bitcast.26), channel_id=1, replica_groups=mesh['sec'=64,'pair'=4] {'sec','pair'}, dimensions={0} | all-to-all | bytes 262144 | tf_op jit(solution)/shard_map/all_to_all | solution.py:283
  107.5 2.6 %terms.7 = (f32[24,128,128]{2,1,0:T(8,128)S(1)}, f32[8,128,128]{2,1,0:T(8,128)S(1)}) custom-call(s32[1]{0:T(128)} %bitcast.group, s32[1]{0:T(128)} %bitcast.1.sector, s32[6]{0:T(128)S(1)} %copy-done.4, f32[1536]{0:T(1024)S(1)} %reshape.54.weights, f32[4,128,128]{2,1,0:T(8,128)S(1)} %get-tuple-element.86.own.corr.refs_8_, ...), custom_call_target="tpu_custom_call" | custom-call | bytes 4194304 | tf_op jit(solution)/shard_map/terms/pallas_call | solution.py:299
  112.7 6.8 %collective-permute-done.10.first = f32[8,128,128]{2,1,0:T(8,128)S(1)} collective-permute-done((f32[8,128,128]{2,1,0:T(8,128)S(1)}, f32[8,128,128]{2,1,0:T(8,128)S(1)}, u32[]{:S(2)}, u32[]{:S(2)}) %collective-permute-start.10) | collective-permute-done | bytes 524320 | tf_op jit(solution)/shard_map/ppermute | solution.py:272
  119.6 5.5 %collective-permute-done.11.second = f32[4,128,128]{2,1,0:T(8,128)S(1)} collective-permute-done((f32[4,128,128]{2,1,0:T(8,128)S(1)}, f32[4,128,128]{2,1,0:T(8,128)S(1)}, u32[]{:S(2)}, u32[]{:S(2)}) %collective-permute-start.11) | collective-permute-done | bytes 262176 | tf_op jit(solution)/shard_map/ppermute | solution.py:272
  125.4 2.8 %collective-permute-start.13 = (f32[4,128,128]{2,1,0:T(8,128)S(1)}, f32[4,128,128]{2,1,0:T(8,128)S(1)}, u32[]{:S(2)}, u32[]{:S(2)}) collective-permute-start(f32[4,128,128]{2,1,0:T(8,128)S(1)} %sum.4.refs_14_), channel_id=1, source_target_pairs={{0,4},{4,0},{8,12},{12,8},{16,20},{20,16},{24,28},{28,24},{32,36},... | collective-permute-start | bytes 786440 | tf_op jit(solution)/shard_map/ppermute | solution.py:278
  128.2 2.1 collective-permute-start.12
  130.3 19.1 %all_to_all.27 = f32[256,1,128]{2,1,0:T(1,128)S(1)} all-to-all(f32[256,1,128]{2,1,0:T(1,128)S(1)} %bitcast.27), channel_id=1, replica_groups=mesh['sec'=64,'pair'=4] {'sec','pair'}, dimensions={0} | all-to-all | bytes 262144 | tf_op jit(solution)/shard_map/all_to_all | solution.py:283
  150.0 2.6 %terms.8 = (f32[24,128,128]{2,1,0:T(8,128)S(1)}, f32[8,128,128]{2,1,0:T(8,128)S(1)}) custom-call(s32[1]{0:T(128)} %bitcast.group, s32[1]{0:T(128)} %bitcast.1.sector, s32[6]{0:T(128)S(1)} %copy-done.4, f32[1536]{0:T(1024)S(1)} %reshape.54.weights, f32[4,128,128]{2,1,0:T(8,128)S(1)} %get-tuple-element.100.own.corr.refs_8_, ...), custom_call_target="tpu_custom_call" | custom-call | bytes 4194304 | tf_op jit(solution)/shard_map/terms/pallas_call | solution.py:299
  155.2 6.8 %collective-permute-done.14.first = f32[8,128,128]{2,1,0:T(8,128)S(1)} collective-permute-done((f32[8,128,128]{2,1,0:T(8,128)S(1)}, f32[8,128,128]{2,1,0:T(8,128)S(1)}, u32[]{:S(2)}, u32[]{:S(2)}) %collective-permute-start.14) | collective-permute-done | bytes 524320 | tf_op jit(solution)/shard_map/ppermute | solution.py:272
  162.1 5.5 %collective-permute-done.15.second = f32[4,128,128]{2,1,0:T(8,128)S(1)} collective-permute-done((f32[4,128,128]{2,1,0:T(8,128)S(1)}, f32[4,128,128]{2,1,0:T(8,128)S(1)}, u32[]{:S(2)}, u32[]{:S(2)}) %collective-permute-start.15) | collective-permute-done | bytes 262176 | tf_op jit(solution)/shard_map/ppermute | solution.py:272
  167.9 2.8 %collective-permute-start.17 = (f32[4,128,128]{2,1,0:T(8,128)S(1)}, f32[4,128,128]{2,1,0:T(8,128)S(1)}, u32[]{:S(2)}, u32[]{:S(2)}) collective-permute-start(f32[4,128,128]{2,1,0:T(8,128)S(1)} %sum.5.refs_14_), channel_id=1, source_target_pairs={{0,4},{4,0},{8,12},{12,8},{16,20},{20,16},{24,28},{28,24},{32,36},... | collective-permute-start | bytes 786440 | tf_op jit(solution)/shard_map/ppermute | solution.py:278
  170.7 2.1 collective-permute-start.16
  172.8 19.1 %all_to_all.28 = f32[256,1,128]{2,1,0:T(1,128)S(1)} all-to-all(f32[256,1,128]{2,1,0:T(1,128)S(1)} %bitcast.28), channel_id=1, replica_groups=mesh['sec'=64,'pair'=4] {'sec','pair'}, dimensions={0} | all-to-all | bytes 262144 | tf_op jit(solution)/shard_map/all_to_all | solution.py:283
  193.3 2.6 %terms.9 = (f32[24,128,128]{2,1,0:T(8,128)S(1)}, f32[8,128,128]{2,1,0:T(8,128)S(1)}) custom-call(s32[1]{0:T(128)} %bitcast.group, s32[1]{0:T(128)} %bitcast.1.sector, s32[6]{0:T(128)S(1)} %copy-done.4, f32[1536]{0:T(1024)S(1)} %reshape.54.weights, f32[4,128,128]{2,1,0:T(8,128)S(1)} %get-tuple-element.114.own.corr.refs_3_, ...), custom_call_target="tpu_custom_call" | custom-call | bytes 4194304 | tf_op jit(solution)/shard_map/terms/pallas_call | solution.py:299
  198.4 6.8 %collective-permute-done.18.first = f32[8,128,128]{2,1,0:T(8,128)S(1)} collective-permute-done((f32[8,128,128]{2,1,0:T(8,128)S(1)}, f32[8,128,128]{2,1,0:T(8,128)S(1)}, u32[]{:S(2)}, u32[]{:S(2)}) %collective-permute-start.18) | collective-permute-done | bytes 524320 | tf_op jit(solution)/shard_map/ppermute | solution.py:272
  205.3 5.5 %collective-permute-done.19.second = f32[4,128,128]{2,1,0:T(8,128)S(1)} collective-permute-done((f32[4,128,128]{2,1,0:T(8,128)S(1)}, f32[4,128,128]{2,1,0:T(8,128)S(1)}, u32[]{:S(2)}, u32[]{:S(2)}) %collective-permute-start.19) | collective-permute-done | bytes 262176 | tf_op jit(solution)/shard_map/ppermute | solution.py:272
  211.1 20.3 %all_to_all.29 = f32[256,1,128]{2,1,0:T(1,128)S(1)} all-to-all(f32[256,1,128]{2,1,0:T(1,128)S(1)} %bitcast.34), channel_id=1, replica_groups=mesh['sec'=64,'pair'=4] {'sec','pair'}, dimensions={0} | all-to-all | bytes 262144 | tf_op jit(solution)/shard_map/all_to_all | solution.py:283
  (56 shorter events, 22.4 us)
Async XLA Ops:
  1.3 1.0 copy-start.2
  2.3 11.5 %collective-permute-start.1 = (f32[4,128,128]{2,1,0:T(8,128)S(1)}, f32[4,128,128]{2,1,0:T(8,128)S(1)}, u32[]{:S(2)}, u32[]{:S(2)}) collective-permute-start(f32[4,128,128]{2,1,0:T(8,128)S(1)} %mask.1.own.state.refs_1_.refs_2_), channel_id=1, source_target_pairs={{0,4},{4,0},{8,12},{12,8},{16,20},{20,16},{24,28},{28,24},{32,36},... | collective-permute-start | bytes 786440 | tf_op jit(solution)/shard_map/ppermute | solution.py:278
  5.6 8.2 %collective-permute-start = (f32[4,128,128]{2,1,0:T(8,128)S(1)}, f32[4,128,128]{2,1,0:T(8,128)S(1)}, u32[]{:S(2)}, u32[]{:S(2)}) collective-permute-start(f32[4,128,128]{2,1,0:T(8,128)S(1)} %mask.1.own.state.refs_1_.refs_2_), channel_id=1, source_target_pairs={{4,8},{8,4},{12,16},{16,12},{20,24},{24,20},{28,32},{32,28},{36,40... | collective-permute-start | bytes 786440 | tf_op jit(solution)/shard_map/ppermute | solution.py:277
  8.4 1.4 copy-start
  9.8 1.0 copy-start.1
  10.8 0.7 copy-start.3
  16.3 9.3 %collective-permute-start.2 = (f32[8,128,128]{2,1,0:T(8,128)S(1)}, f32[8,128,128]{2,1,0:T(8,128)S(1)}, u32[]{:S(2)}, u32[]{:S(2)}) collective-permute-start(f32[8,128,128]{2,1,0:T(8,128)S(1)} %get-tuple-element.68), channel_id=1, source_target_pairs={{0,1},{1,0},{2,3},{3,2},{4,7},{5,6},{6,5},{7,4},{8,9},{9,8},{10,11... | collective-permute-start | bytes 1572872 | tf_op jit(solution)/shard_map/ppermute | solution.py:272
  25.7 5.6 %collective-permute-start.3 = (f32[4,128,128]{2,1,0:T(8,128)S(1)}, f32[4,128,128]{2,1,0:T(8,128)S(1)}, u32[]{:S(2)}, u32[]{:S(2)}) collective-permute-start(f32[4,128,128]{2,1,0:T(8,128)S(1)} %onward.5), channel_id=1, source_target_pairs={{0,3},{1,2},{2,1},{3,0},{4,5},{5,4},{6,7},{7,6},{8,11},{9,10},{10,... | collective-permute-start | bytes 786440 | tf_op jit(solution)/shard_map/ppermute | solution.py:272
  31.5 32.5 %collective-permute-start.5 = (f32[520,128]{1,0:T(8,128)S(1)}, f32[520,128]{1,0:T(8,128)S(1)}, u32[]{:S(2)}, u32[]{:S(2)}) collective-permute-start(f32[520,128]{1,0:T(8,128)S(1)} %first_sum.1.refs_4_), channel_id=1, source_target_pairs={{0,4},{4,0},{8,12},{12,8},{16,20},{20,16},{24,28},{28,24},{32,36},... | collective-permute-start | bytes 798728 | tf_op jit(solution)/shard_map/ppermute | solution.py:278
  32.4 31.6 %collective-permute-start.4 = (f32[520,128]{1,0:T(8,128)S(1)}, f32[520,128]{1,0:T(8,128)S(1)}, u32[]{:S(2)}, u32[]{:S(2)}) collective-permute-start(f32[520,128]{1,0:T(8,128)S(1)} %first_sum.1.refs_4_), channel_id=1, source_target_pairs={{4,8},{8,4},{12,16},{16,12},{20,24},{24,20},{28,32},{32,28},{36,40... | collective-permute-start | bytes 798728 | tf_op jit(solution)/shard_map/ppermute | solution.py:277
  67.4 9.5 %collective-permute-start.6 = (f32[8,128,128]{2,1,0:T(8,128)S(1)}, f32[8,128,128]{2,1,0:T(8,128)S(1)}, u32[]{:S(2)}, u32[]{:S(2)}) collective-permute-start(f32[8,128,128]{2,1,0:T(8,128)S(1)} %get-tuple-element.78), channel_id=1, source_target_pairs={{0,1},{1,0},{2,3},{3,2},{4,7},{5,6},{6,5},{7,4},{8,9},{9,8},{10,11... | collective-permute-start | bytes 1572872 | tf_op jit(solution)/shard_map/ppermute | solution.py:272
  76.9 5.6 %collective-permute-start.7 = (f32[4,128,128]{2,1,0:T(8,128)S(1)}, f32[4,128,128]{2,1,0:T(8,128)S(1)}, u32[]{:S(2)}, u32[]{:S(2)}) collective-permute-start(f32[4,128,128]{2,1,0:T(8,128)S(1)} %onward.6), channel_id=1, source_target_pairs={{0,3},{1,2},{2,1},{3,0},{4,5},{5,4},{6,7},{7,6},{8,11},{9,10},{10,... | collective-permute-start | bytes 786440 | tf_op jit(solution)/shard_map/ppermute | solution.py:272
  82.8 24.1 %collective-permute-start.9 = (f32[4,128,128]{2,1,0:T(8,128)S(1)}, f32[4,128,128]{2,1,0:T(8,128)S(1)}, u32[]{:S(2)}, u32[]{:S(2)}) collective-permute-start(f32[4,128,128]{2,1,0:T(8,128)S(1)} %sum.3.refs_14_), channel_id=1, source_target_pairs={{0,4},{4,0},{8,12},{12,8},{16,20},{20,16},{24,28},{28,24},{32,36},... | collective-permute-start | bytes 786440 | tf_op jit(solution)/shard_map/ppermute | solution.py:278
  85.6 21.2 %collective-permute-start.8 = (f32[4,128,128]{2,1,0:T(8,128)S(1)}, f32[4,128,128]{2,1,0:T(8,128)S(1)}, u32[]{:S(2)}, u32[]{:S(2)}) collective-permute-start(f32[4,128,128]{2,1,0:T(8,128)S(1)} %sum.3.refs_14_), channel_id=1, source_target_pairs={{4,8},{8,4},{12,16},{16,12},{20,24},{24,20},{28,32},{32,28},{36,40... | collective-permute-start | bytes 786440 | tf_op jit(solution)/shard_map/ppermute | solution.py:277
  106.9 0.7 copy-start.4
  110.1 9.3 %collective-permute-start.10 = (f32[8,128,128]{2,1,0:T(8,128)S(1)}, f32[8,128,128]{2,1,0:T(8,128)S(1)}, u32[]{:S(2)}, u32[]{:S(2)}) collective-permute-start(f32[8,128,128]{2,1,0:T(8,128)S(1)} %get-tuple-element.91), channel_id=1, source_target_pairs={{0,1},{1,0},{2,3},{3,2},{4,7},{5,6},{6,5},{7,4},{8,9},{9,8},{10,11... | collective-permute-start | bytes 1572872 | tf_op jit(solution)/shard_map/ppermute | solution.py:272
  119.5 5.6 %collective-permute-start.11 = (f32[4,128,128]{2,1,0:T(8,128)S(1)}, f32[4,128,128]{2,1,0:T(8,128)S(1)}, u32[]{:S(2)}, u32[]{:S(2)}) collective-permute-start(f32[4,128,128]{2,1,0:T(8,128)S(1)} %onward.7), channel_id=1, source_target_pairs={{0,3},{1,2},{2,1},{3,0},{4,5},{5,4},{6,7},{7,6},{8,11},{9,10},{10,... | collective-permute-start | bytes 786440 | tf_op jit(solution)/shard_map/ppermute | solution.py:272
  125.4 24.1 %collective-permute-start.13 = (f32[4,128,128]{2,1,0:T(8,128)S(1)}, f32[4,128,128]{2,1,0:T(8,128)S(1)}, u32[]{:S(2)}, u32[]{:S(2)}) collective-permute-start(f32[4,128,128]{2,1,0:T(8,128)S(1)} %sum.4.refs_14_), channel_id=1, source_target_pairs={{0,4},{4,0},{8,12},{12,8},{16,20},{20,16},{24,28},{28,24},{32,36},... | collective-permute-start | bytes 786440 | tf_op jit(solution)/shard_map/ppermute | solution.py:278
  128.2 21.2 %collective-permute-start.12 = (f32[4,128,128]{2,1,0:T(8,128)S(1)}, f32[4,128,128]{2,1,0:T(8,128)S(1)}, u32[]{:S(2)}, u32[]{:S(2)}) collective-permute-start(f32[4,128,128]{2,1,0:T(8,128)S(1)} %sum.4.refs_14_), channel_id=1, source_target_pairs={{4,8},{8,4},{12,16},{16,12},{20,24},{24,20},{28,32},{32,28},{36,40... | collective-permute-start | bytes 786440 | tf_op jit(solution)/shard_map/ppermute | solution.py:277
  152.6 9.3 %collective-permute-start.14 = (f32[8,128,128]{2,1,0:T(8,128)S(1)}, f32[8,128,128]{2,1,0:T(8,128)S(1)}, u32[]{:S(2)}, u32[]{:S(2)}) collective-permute-start(f32[8,128,128]{2,1,0:T(8,128)S(1)} %get-tuple-element.105), channel_id=1, source_target_pairs={{0,1},{1,0},{2,3},{3,2},{4,7},{5,6},{6,5},{7,4},{8,9},{9,8},{10,11... | collective-permute-start | bytes 1572872 | tf_op jit(solution)/shard_map/ppermute | solution.py:272
  162.0 5.6 %collective-permute-start.15 = (f32[4,128,128]{2,1,0:T(8,128)S(1)}, f32[4,128,128]{2,1,0:T(8,128)S(1)}, u32[]{:S(2)}, u32[]{:S(2)}) collective-permute-start(f32[4,128,128]{2,1,0:T(8,128)S(1)} %onward.8), channel_id=1, source_target_pairs={{0,3},{1,2},{2,1},{3,0},{4,5},{5,4},{6,7},{7,6},{8,11},{9,10},{10,... | collective-permute-start | bytes 786440 | tf_op jit(solution)/shard_map/ppermute | solution.py:272
  167.9 24.1 %collective-permute-start.17 = (f32[4,128,128]{2,1,0:T(8,128)S(1)}, f32[4,128,128]{2,1,0:T(8,128)S(1)}, u32[]{:S(2)}, u32[]{:S(2)}) collective-permute-start(f32[4,128,128]{2,1,0:T(8,128)S(1)} %sum.5.refs_14_), channel_id=1, source_target_pairs={{0,4},{4,0},{8,12},{12,8},{16,20},{20,16},{24,28},{28,24},{32,36},... | collective-permute-start | bytes 786440 | tf_op jit(solution)/shard_map/ppermute | solution.py:278
  170.7 21.3 %collective-permute-start.16 = (f32[4,128,128]{2,1,0:T(8,128)S(1)}, f32[4,128,128]{2,1,0:T(8,128)S(1)}, u32[]{:S(2)}, u32[]{:S(2)}) collective-permute-start(f32[4,128,128]{2,1,0:T(8,128)S(1)} %sum.5.refs_14_), channel_id=1, source_target_pairs={{4,8},{8,4},{12,16},{16,12},{20,24},{24,20},{28,32},{32,28},{36,40... | collective-permute-start | bytes 786440 | tf_op jit(solution)/shard_map/ppermute | solution.py:277
  195.9 9.3 %collective-permute-start.18 = (f32[8,128,128]{2,1,0:T(8,128)S(1)}, f32[8,128,128]{2,1,0:T(8,128)S(1)}, u32[]{:S(2)}, u32[]{:S(2)}) collective-permute-start(f32[8,128,128]{2,1,0:T(8,128)S(1)} %get-tuple-element.119), channel_id=1, source_target_pairs={{0,1},{1,0},{2,3},{3,2},{4,7},{5,6},{6,5},{7,4},{8,9},{9,8},{10,11... | collective-permute-start | bytes 1572872 | tf_op jit(solution)/shard_map/ppermute | solution.py:272
  205.2 5.6 %collective-permute-start.19 = (f32[4,128,128]{2,1,0:T(8,128)S(1)}, f32[4,128,128]{2,1,0:T(8,128)S(1)}, u32[]{:S(2)}, u32[]{:S(2)}) collective-permute-start(f32[4,128,128]{2,1,0:T(8,128)S(1)} %onward.9), channel_id=1, source_target_pairs={{0,3},{1,2},{2,1},{3,0},{4,5},{5,4},{6,7},{7,6},{8,11},{9,10},{10,... | collective-permute-start | bytes 786440 | tf_op jit(solution)/shard_map/ppermute | solution.py:272
